TPU v7x, 32 devices: a whole 2x2x4 slice. The times are simulated.
32 devices in a mesh: dp: 16 (over z, y, core), mp: 2 (over x).
Axes of the slice: x: 2, y: 2, z: 4, core: 2. Of those that a mesh axis runs over, the one named last changes fastest.
Arguments:
- inputs: float32 [128, 384, 384], P('dp'), may hold values from -6 to 6
- out_grad: float32 [128, 384, 384], P('dp'), may hold values from -6 to 6
- counts: int32 [128], P('dp'), may hold values from 32 to 128, as said below
- qkv_weight: float32 [3, 384, 384], P(None, 'dp', 'mp'), may hold values from -0.3125 to 0.3125
- out_weight: float32 [384, 384], P('mp', 'dp'), may hold values from -3 to 3
- up_weight: float32 [384, 1536], P('dp', 'mp'), may hold values from -0.3125 to 0.3125
- down_weight: float32 [1536, 384], P('mp', 'dp'), may hold values from -0.15625 to 0.15625
- norm_vectors: float32 [2, 384], P(None, 'dp'), may hold values from 0.55 to 1.45, as said below
- qkv_first: float32 [3, 384, 384], P(None, 'dp', 'mp'), may hold values from -640 to 640
- out_first: float32 [384, 384], P('mp', 'dp'), may hold values from -128 to 128
- up_first: float32 [384, 1536], P('dp', 'mp'), may hold values from -384 to 384
- down_first: float32 [1536, 384], P('mp', 'dp'), may hold values from -640 to 640
- norm_first: float32 [2, 384], P(None, 'dp'), may hold values from -640 to 640
- qkv_second: float32 [3, 384, 384], P(None, 'dp', 'mp'), may hold values from 12288 to 49152
- out_second: float32 [384, 384], P('mp', 'dp'), may hold values from 491.52 to 1966.08
- up_second: float32 [384, 1536], P('dp', 'mp'), may hold values from 4423.68 to 17694.72
- down_second: float32 [1536, 384], P('mp', 'dp'), may hold values from 12288 to 49152
- norm_second: float32 [2, 384], P(None, 'dp'), may hold values from 12288 to 49152
Outputs:
- block_out: float32 [128, 384, 384], P('dp')
- input_grad: float32 [128, 384, 384], P('dp')
- qkv_new: float32 [3, 384, 384], P(None, 'dp', 'mp')
- out_new: float32 [384, 384], P('mp', 'dp')
- up_new: float32 [384, 1536], P('dp', 'mp')
- down_new: float32 [1536, 384], P('mp', 'dp')
- norm_vectors_updated: float32 [2, 384], P(None, 'dp')
- qkv_first_new: float32 [3, 384, 384], P(None, 'dp', 'mp')
- out_first_new: float32 [384, 384], P('mp', 'dp')
- up_first_new: float32 [384, 1536], P('dp', 'mp')
- down_first_new: float32 [1536, 384], P('mp', 'dp')
- norm_first_new: float32 [2, 384], P(None, 'dp')
- qkv_second_new: float32 [3, 384, 384], P(None, 'dp', 'mp')
- out_second_new: float32 [384, 384], P('mp', 'dp')
- up_second_new: float32 [384, 1536], P('dp', 'mp')
- down_second_new: float32 [1536, 384], P('mp', 'dp')
- norm_second_new: float32 [2, 384], P(None, 'dp')
- qkv_grad_sum: float32 [3, 384, 384], P(None, 'dp', 'mp')
- out_grad_sum: float32 [384, 384], P('mp', 'dp')
- up_grad_sum: float32 [384, 1536], P('dp', 'mp')
- down_grad_sum: float32 [1536, 384], P('mp', 'dp')
- norm_grad_sum: float32 [2, 384], P(None, 'dp')
Inputs may be any that keep to these rules, and one draw needn't show every extreme that they name: `counts`: each image's count is a quarter, a half or all of 128; every draw holds both a full and a quarter count. `norm_vectors`: both rows are gains near one.
All inputs are finite; a program needn't handle non-finite values.
Results may differ from a plain program's by a relative error of at most 0.013.
The roundings to bfloat16 on the way count: a program that leaves them out, or rounds other values in their place, can miss the bound.
Values may be sent and summed in bfloat16 or wider, within the bound.
A program may use at most 128 MiB of HBM per device.

v0:
```python
from functools import partial

import jax
import jax.numpy as jnp
from jax import lax
from jax.sharding import PartitionSpec as P

D = 384
HEAD_DIM = 64
PATCHES = 256
STEP = 5


EPS_NORM = 1e-06
EPS_ADAM = 1e-08
BETA_FIRST = 0.5
BETA_SECOND = 0.5
DECAY_MATRIX = 0.01
RATE_QKV = 0.05
RATE_OUT = 0.2
RATE_UP = 0.05
RATE_DOWN = 0.03
RATE_NORM = 0.3


def layer_norm(activations, gain_row):
    center = jnp.mean(activations, axis=-1, keepdims=True)
    shifted = activations - center
    spread = jnp.mean(shifted * shifted, axis=-1, keepdims=True)
    return shifted * lax.rsqrt(spread + EPS_NORM) * gain_row


def attention_part(image_rows, counts, weight_heads, gain_row):
    normed = layer_norm(image_rows, gain_row).astype(jnp.bfloat16)
    projected = jnp.einsum(
        "bsd,cdhe->cbhse", normed, weight_heads, preferred_element_type=jnp.float32
    ).astype(jnp.bfloat16)
    query_rows, key_rows, value_rows = (projected[0], projected[1], projected[2])
    raw_scores = jnp.einsum(
        "bhqe,bhke->bhqk", query_rows, key_rows, preferred_element_type=jnp.float32
    ) * HEAD_DIM ** (-0.5)
    seq_len = image_rows.shape[1]
    key_index = lax.broadcasted_iota(jnp.int32, (1, 1, 1, seq_len), 3)
    live_keys = key_index < (PATCHES + counts)[:, None, None, None]
    masked = jnp.where(live_keys, raw_scores, -1e30)
    row_top = jnp.max(masked, axis=-1, keepdims=True)
    exponent = jnp.exp(masked - row_top)
    probs_full = exponent / jnp.sum(exponent, axis=-1, keepdims=True)
    probs_low = probs_full.astype(jnp.bfloat16)
    blended_heads = jnp.einsum(
        "bhqk,bhke->bhqe", probs_low, value_rows, preferred_element_type=jnp.float32
    ).astype(jnp.bfloat16)
    return (normed, query_rows, key_rows, value_rows, probs_full, probs_low, blended_heads)


def feed_part(middle, full_up, gain_row):
    normed_two = layer_norm(middle, gain_row).astype(jnp.bfloat16)
    hidden = jnp.einsum("bsd,df->bsf", normed_two, full_up, preferred_element_type=jnp.float32)
    active = jax.nn.gelu(hidden, approximate=False).astype(jnp.bfloat16)
    return (normed_two, hidden, active)


def adamw_update(weight, gradient, first_moment, second_moment, step_rate, decay_rate):
    first_next = BETA_FIRST * first_moment + (1.0 - BETA_FIRST) * gradient
    second_next = BETA_SECOND * second_moment + (1.0 - BETA_SECOND) * gradient * gradient
    first_fixed = first_next / (1.0 - BETA_FIRST**STEP)
    second_fixed = second_next / (1.0 - BETA_SECOND**STEP)
    weight_next = weight - step_rate * (
        first_fixed / (jnp.sqrt(second_fixed) + EPS_ADAM) + decay_rate * weight
    )
    return (weight_next, first_next, second_next)


def shards(
    inputs,
    out_grad,
    counts,
    qkv_weight,
    out_weight,
    up_weight,
    down_weight,
    norm_vectors,
    qkv_first,
    out_first,
    up_first,
    down_first,
    norm_first,
    qkv_second,
    out_second,
    up_second,
    down_second,
    norm_second,
):
    full_qkv, full_out, full_up, full_down, full_norm = (
        lax.all_gather(qkv_weight.astype(jnp.bfloat16), "dp", axis=1, tiled=True),
        lax.all_gather(out_weight.astype(jnp.bfloat16), "dp", axis=1, tiled=True),
        lax.all_gather(up_weight.astype(jnp.bfloat16), "dp", axis=0, tiled=True),
        lax.all_gather(down_weight.astype(jnp.bfloat16), "dp", axis=1, tiled=True),
        lax.all_gather(norm_vectors.astype(jnp.bfloat16), "dp", axis=1, tiled=True),
    )
    norm_params = full_norm.astype(jnp.float32)
    heads_here = full_qkv.shape[2] // HEAD_DIM
    weight_heads = full_qkv.reshape(3, D, heads_here, HEAD_DIM)
    output_heads = full_out.reshape(heads_here, HEAD_DIM, D)
    attention_output = attention_part(inputs, counts, weight_heads, norm_params[0])
    branch = jnp.einsum(
        "uvsa,vay->usy", attention_output[6], output_heads, preferred_element_type=jnp.float32
    )
    middle = inputs + lax.psum(branch, "mp")
    feedforward_state = feed_part(middle, full_up, norm_params[1])
    feed_term = jnp.einsum(
        "bsf,fd->bsd", feedforward_state[2], full_down, preferred_element_type=jnp.float32
    )
    block_out = middle + lax.psum(feed_term.astype(jnp.bfloat16), "mp").astype(jnp.float32)
    attention_output = attention_part(inputs, counts, weight_heads, norm_params[0])
    feedforward_state = feed_part(middle, full_up, norm_params[1])
    normed_two, hidden, active = feedforward_state
    normed, query_rows, key_rows, value_rows, probs_full, probs_low, blended_heads = (
        attention_output
    )
    grad_low = out_grad.astype(jnp.bfloat16)
    down_grad = jnp.einsum("bsf,bsd->fd", active, grad_low, preferred_element_type=jnp.float32)
    grad_active = jnp.einsum("bsd,fd->bsf", grad_low, full_down, preferred_element_type=jnp.float32)
    gelu_value, gelu_pull = jax.vjp(partial(jax.nn.gelu, approximate=False), hidden)
    grad_hidden = gelu_pull(grad_active)[0].astype(jnp.bfloat16)
    up_grad = jnp.einsum("bsd,bsf->df", normed_two, grad_hidden, preferred_element_type=jnp.float32)
    part_two = jnp.einsum("bsf,df->bsd", grad_hidden, full_up, preferred_element_type=jnp.float32)
    grad_normed_two = lax.psum(part_two, "mp")
    norm_value, norm_pullback = jax.vjp(layer_norm, middle, norm_params[1])
    grad_middle_norm, grad_gain_two = norm_pullback(grad_normed_two)
    grad_middle = out_grad + grad_middle_norm
    branch_gradient = grad_middle.astype(jnp.bfloat16)
    out_grad_w = jnp.einsum(
        "gcap,gax->cpx", blended_heads, branch_gradient, preferred_element_type=jnp.float32
    ).reshape(heads_here * HEAD_DIM, D)
    grad_mixed = jnp.einsum(
        "ran,oin->roai", branch_gradient, output_heads, preferred_element_type=jnp.float32
    ).astype(jnp.bfloat16)
    grad_value = jnp.einsum(
        "bhqk,bhqe->bhke", probs_low, grad_mixed, preferred_element_type=jnp.float32
    ).astype(jnp.bfloat16)
    grad_probs = jnp.einsum(
        "bhqe,bhke->bhqk", grad_mixed, value_rows, preferred_element_type=jnp.float32
    )
    row_inner = jnp.sum(probs_full * grad_probs, axis=-1, keepdims=True)
    grad_scores = (probs_full * (grad_probs - row_inner)).astype(jnp.bfloat16)
    score_scale = HEAD_DIM ** (-0.5)
    grad_query = (
        jnp.einsum("bhqk,bhke->bhqe", grad_scores, key_rows, preferred_element_type=jnp.float32)
        * score_scale
    ).astype(jnp.bfloat16)
    grad_key = (
        jnp.einsum("bhqk,bhqe->bhke", grad_scores, query_rows, preferred_element_type=jnp.float32)
        * score_scale
    ).astype(jnp.bfloat16)
    stacked = jnp.stack([grad_query, grad_key, grad_value])
    qkv_grad = jnp.einsum(
        "cbhse,bsd->cdhe", stacked, normed, preferred_element_type=jnp.float32
    ).reshape(3, D, heads_here * HEAD_DIM)
    part_one = jnp.einsum(
        "cbhse,cdhe->bsd", stacked, weight_heads, preferred_element_type=jnp.float32
    )
    grad_normed_one = lax.psum(part_one.astype(jnp.bfloat16), "mp").astype(jnp.float32)
    first_value, first_pull = jax.vjp(layer_norm, inputs, norm_params[0])
    grad_input_norm, grad_gain_one = first_pull(grad_normed_one)
    input_grad = grad_middle + grad_input_norm
    norm_grad = jnp.stack([grad_gain_one, grad_gain_two])
    all_grads = (qkv_grad, out_grad_w, up_grad, down_grad, norm_grad)
    totals = lax.psum((all_grads[0], all_grads[1], all_grads[2], all_grads[3], all_grads[4]), "dp")
    position = lax.axis_index("dp")
    own_grads = (
        lax.dynamic_slice_in_dim(totals[0], position * qkv_weight.shape[1], qkv_weight.shape[1], 1),
        lax.dynamic_slice_in_dim(totals[1], position * out_weight.shape[1], out_weight.shape[1], 1),
        lax.dynamic_slice_in_dim(totals[2], position * up_weight.shape[0], up_weight.shape[0], 0),
        lax.dynamic_slice_in_dim(
            totals[3], position * down_weight.shape[1], down_weight.shape[1], 1
        ),
        lax.dynamic_slice_in_dim(
            totals[4], position * norm_vectors.shape[1], norm_vectors.shape[1], 1
        ),
    )
    qkv_new, qkv_first_new, qkv_second_new = adamw_update(
        qkv_weight, own_grads[0], qkv_first, qkv_second, RATE_QKV, DECAY_MATRIX
    )
    out_new, out_first_new, out_second_new = adamw_update(
        out_weight, own_grads[1], out_first, out_second, RATE_OUT, DECAY_MATRIX
    )
    up_new, up_first_new, up_second_new = adamw_update(
        up_weight, own_grads[2], up_first, up_second, RATE_UP, DECAY_MATRIX
    )
    down_new, down_first_new, down_second_new = adamw_update(
        down_weight, own_grads[3], down_first, down_second, RATE_DOWN, DECAY_MATRIX
    )
    norm_vectors_updated, norm_first_new, norm_second_new = adamw_update(
        norm_vectors, own_grads[4], norm_first, norm_second, RATE_NORM, 0.0
    )
    return (
        block_out,
        input_grad,
        qkv_new,
        out_new,
        up_new,
        down_new,
        norm_vectors_updated,
        qkv_first_new,
        out_first_new,
        up_first_new,
        down_first_new,
        norm_first_new,
        qkv_second_new,
        out_second_new,
        up_second_new,
        down_second_new,
        norm_second_new,
        own_grads[0],
        own_grads[1],
        own_grads[2],
        own_grads[3],
        own_grads[4],
    )


def solution(mesh):
    in_specs = (
        P("dp", None, None),
        P("dp", None, None),
        P("dp"),
        P(None, "dp", "mp"),
        P("mp", "dp"),
        P("dp", "mp"),
        P("mp", "dp"),
        P(None, "dp"),
        P(None, "dp", "mp"),
        P("mp", "dp"),
        P("dp", "mp"),
        P("mp", "dp"),
        P(None, "dp"),
        P(None, "dp", "mp"),
        P("mp", "dp"),
        P("dp", "mp"),
        P("mp", "dp"),
        P(None, "dp"),
    )
    out_specs = (
        P("dp", None, None),
        P("dp", None, None),
        P(None, "dp", "mp"),
        P("mp", "dp"),
        P("dp", "mp"),
        P("mp", "dp"),
        P(None, "dp"),
        P(None, "dp", "mp"),
        P("mp", "dp"),
        P("dp", "mp"),
        P("mp", "dp"),
        P(None, "dp"),
        P(None, "dp", "mp"),
        P("mp", "dp"),
        P("dp", "mp"),
        P("mp", "dp"),
        P(None, "dp"),
        P(None, "dp", "mp"),
        P("mp", "dp"),
        P("dp", "mp"),
        P("mp", "dp"),
        P(None, "dp"),
    )
    return jax.shard_map(shards, mesh=mesh, in_specs=in_specs, out_specs=out_specs, check_vma=False)
```

profile of v0, /device:TPU:0, one launch (start us, length us, event | category | flops | bytes accessed | tf_op | source)
XLA Modules:
  0.0 736.9 jit_solution(17295481404064817658)
XLA Ops:
  7.2 0.0 all-reduce.7.cloned.1.call-start
  7.2 0.7 broadcast_add_fusion
  7.9 0.7 convert_bitcast_fusion.1
  8.6 0.1 iota_compare_fusion
  8.7 23.0 %all-gather = bf16[16,24,2]{1,2,0:T(2,128)(2,1)S(1)} all-gather(bf16[1,24,2]{1,2,0:T(2,128)(2,1)S(1)} %convert_bitcast_fusion.1), channel_id=1, replica_groups=mesh['dp'=16,'mp'=2] {'dp'}, dimensions={0}, use_global_device_ids=true | all-gather | bytes 1632 | tf_op jit(solution)/shard_map/all_gather | solution.py:99
  31.6 0.1 reshape.144
  31.7 0.7 convert_element_type.92
  32.5 2.8 reduce_sum.105
  35.4 3.2 multiply_reduce_fusion.4
  38.6 17.9 %all_gather.17 = bf16[192,384]{0,1:T(8,128)(2,1)S(1)} all-gather(bf16[192,24]{0,1:T(8,128)(2,1)S(1)} %convert_element_type.92), channel_id=1, replica_groups=mesh['dp'=16,'mp'=2] {'dp'}, dimensions={1}, use_global_device_ids=true | all-gather | bytes 156672 | tf_op jit(solution)/shard_map/all_gather | solution.py:96
  56.6 0.1 copy.82
  56.7 20.5 %all_gather.16 = bf16[3,384,192]{2,1,0:T(8,128)(2,1)S(1)} all-gather(bf16[3,24,192]{2,1,0:T(8,128)(2,1)S(1)} %convert_element_type.87), channel_id=1, replica_groups=mesh['dp'=16,'mp'=2] {'dp'}, dimensions={1}, use_global_device_ids=true | all-gather | bytes 470016 | tf_op jit(solution)/shard_map/all_gather | solution.py:95
  77.2 0.3 copy.80
  77.5 6.4 convert_bitcast_fusion
  83.9 9.5 %fusion.78 = (f32[8,3,384]{2,1,0:T(4,128)S(1)}, f32[8,3,384,384]{2,3,1,0:T(8,128)}) fusion(pred[8,384]{1,0:T(8,128)(4,1)S(1)} %iota_compare_fusion, bf16[3,8,3,384,64]{3,4,2,0,1:T(8,128)(2,1)} %convert_bitcast_fusion), kind=kOutput, calls=%fused_computation.141 | convolution fusion | flops 467140992 | bytes 16555008 | tf_op jit(solution)/shard_map/sub | solution.py:47
  93.5 7.7 %fusion.35 = bf16[8,3,384,64]{2,3,1,0:T(8,128)(2,1)S(1)} fusion(bf16[3,8,3,384,64]{3,4,2,0,1:T(8,128)(2,1)} %convert_bitcast_fusion, f32[8,3,384]{2,1,0:T(4,128)S(1)} %get-tuple-element.62, pred[8,384]{1,0:T(8,128)(4,1)S(1)} %iota_compare_fusion), kind=kOutput, calls=%fused_computation.72 | convolution fusion | flops 924263808 | bytes 4758528 | tf_op jit(solution)/shard_map/bhqk,bhke->bhqe/dot_general | solution.py:50
  101.2 3.2 convolution_bitcast_fusion
  104.4 0.0 all-reduce.7.cloned.1.call-update
  104.4 0.0 all-reduce.9.cloned.1.call-start
  104.5 19.1 %all_gather.19 = bf16[768,384]{0,1:T(8,128)(2,1)S(1)} all-gather(bf16[768,24]{0,1:T(8,128)(2,1)S(1)} %convert_element_type.96), channel_id=1, replica_groups=mesh['dp'=16,'mp'=2] {'dp'}, dimensions={1}, use_global_device_ids=true | all-gather | bytes 626688 | tf_op jit(solution)/shard_map/all_gather | solution.py:98
  123.6 20.8 %all_gather.18 = bf16[384,768]{1,0:T(8,128)(2,1)S(1)} all-gather(bf16[24,768]{1,0:T(8,128)(2,1)S(1)} %convert_element_type.94), channel_id=1, replica_groups=mesh['dp'=16,'mp'=2] {'dp'}, dimensions={0}, use_global_device_ids=true | all-gather | bytes 626688 | tf_op jit(solution)/shard_map/all_gather | solution.py:97
  144.4 76.6 %all-reduce.7.cloned.1.call-done = f32[8,384,384]{2,1,0:T(8,128)} async-done(((f32[8,384,384]{2,1,0:T(8,128)}), f32[8,384,384]{2,1,0:T(8,128)}) %all-reduce.7.cloned.1.call-update) | async-done | bytes 4718608 | tf_op jit(solution)/shard_map/psum | solution.py:109
  221.0 4.3 fusion.77
  225.4 0.9 multiply_reduce_fusion.3
  226.3 5.2 fusion.27
  231.6 22.3 %multiply_convert_fusion.1 = (bf16[8,384,768]{2,1,0:T(8,128)(2,1)}, f32[8,384,768]{2,1,0:T(8,128)}) fusion(f32[8,384,768]{2,1,0:T(8,128)S(1)} %get-tuple-element.64, u8[384,768]{1,0:T(8,128)(4,1)S(1)} %get-tuple-element.25, u8[384,768]{1,0:T(8,128)(4,1)S(1)} %get-tuple-element.24), kind=kLoop, calls=%fused_computation.14 | loop fusion | flops 165150720 | bytes 24182784 | tf_op jit(solution)/shard_map/convert_element_type | solution.py:59
  253.9 8.9 %add_convert_fusion = bf16[8,384,768]{2,1,0:T(8,128)(2,1)} fusion(f32[8,384,768]{2,1,0:T(8,128)} %get-tuple-element.59, f32[8,384,768]{2,1,0:T(8,128)S(1)} %get-tuple-element.64, f32[8,384,384]{2,1,0:T(8,128)S(1)} %bitcast.140, bf16[768,384]{0,1:T(8,128)(2,1)S(1)} %all_gather.19), kind=kOutput, calls=%fused_computation.13 | convolution fusion | flops 1846149120 | bytes 28901376 | tf_op jit(solution)/shard_map/bsd,fd->bsf/dot_general | solution.py:123
  262.8 7.1 fusion.55
  270.0 0.0 all-reduce.11.cloned.1.call-start
  270.0 7.0 convolution_bitcast_fusion.1
  277.0 5.9 convolution_bitcast_fusion.2
  282.9 106.4 %all-reduce.9.cloned.1.call-done = f32[8,384,384]{2,1,0:T(8,128)} async-done(((f32[8,384,384]{2,1,0:T(8,128)}), f32[8,384,384]{2,1,0:T(8,128)}) %all-reduce.9.cloned.1.call-update) | async-done | bytes 4718608 | tf_op jit(solution)/shard_map/psum | solution.py:128
  389.3 4.9 multiply_reduce_fusion.1
  394.3 0.1 copy-done.3
  394.4 4.5 fusion.75
  399.0 0.7 fusion.31
  399.7 1.4 copy-done.1
  401.1 0.8 fusion.22
  401.9 1.0 fusion.44
  402.9 8.3 %fusion.41 = bf16[1,8,3,384,64]{3,4,2,1,0:T(8,128)(2,1)} fusion(bf16[8,3,384,64]{2,3,1,0:T(8,128)(2,1)S(1)} %fusion.44, f32[8,3,384]{2,1,0:T(4,128)S(1)} %copy-done.21, pred[8,384]{1,0:T(8,128)(4,1)S(1)} %iota_compare_fusion, bf16[3,8,3,384,64]{3,4,2,0,1:T(8,128)(2,1)} %convert_bitcast_fusion), kind=kOutput, calls=%fused_computation.76 | convolution fusion | flops 924263808 | bytes 4758528 | tf_op jit(solution)/shard_map/bhqk,bhqe->bhke/dot_general | solution.py:139
  411.1 13.0 %multiply_reduce_fusion = (f32[8,3,384]{2,1,0:T(4,128)S(1)}, f32[8,3,384,384]{2,3,1,0:T(8,128)}) fusion(f32[8,3,384,384]{2,3,1,0:T(8,128)} %get-tuple-element.63, f32[8,3,384]{2,1,0:T(4,128)S(1)} %copy-done.21, bf16[8,3,384,64]{2,3,1,0:T(8,128)(2,1)S(1)} %fusion.44, bf16[3,8,3,384,64]{3,4,2,0,1:T(8,128)(2,1)} %convert_bitcast_fusion), kind=kOutput, calls=%fused_computation.2 | convolution fusion | flops 463592448 | bytes 30744576 | tf_op jit(solution)/shard_map/bhqe,bhke->bhqk/dot_general | solution.py:142
  424.1 10.3 %multiply_convert_fusion = bf16[8,3,384,384]{2,3,1,0:T(8,128)(2,1)S(1)} fusion(f32[8,3,384,384]{2,3,1,0:T(8,128)} %get-tuple-element.66, f32[8,3,384]{2,1,0:T(4,128)S(1)} %get-tuple-element.65, f32[8,3,384,384]{2,3,1,0:T(8,128)} %get-tuple-element.63, f32[8,3,384]{2,1,0:T(4,128)S(1)} %copy-done.21), kind=kLoop, calls=%fused_computation.1 | loop fusion | flops 14155776 | bytes 35463168 | tf_op jit(solution)/shard_map/convert_element_type | solution.py:146
  434.4 3.6 fusion.48
  438.1 1.3 fusion.47
  439.4 0.9 copy.88
  440.3 5.1 fusion.19
  445.4 1.4 copy.87
  446.9 0.0 all-reduce.13.cloned.1.call-start
  446.9 6.6 convolution_convert_fusion
  453.5 3.8 bitcast_convert_fusion
  457.4 0.0 all-reduce.13.cloned.1.call-update
  457.4 99.3 %all-reduce.11.cloned.1.call-done = (f32[3,384,192]{2,1,0:T(8,128)}, f32[192,384]{0,1:T(8,128)}, f32[384,768]{1,0:T(8,128)}, f32[768,384]{0,1:T(8,128)}) async-done(((f32[3,384,192]{2,1,0:T(8,128)}, f32[192,384]{0,1:T(8,128)}, f32[384,768]{1,0:T(8,128)}, f32[768,384]{0,1:T(8,128)}), (f32[3,384,192]{2,1,0:T(8,128)}, f32[192,384]{0,1:T(8,128)}, f32[384,768]{1,0:T(8,128)}, ...) | async-done | bytes 3538960 | tf_op jit(solution)/shard_map/psum | solution.py:169
  556.8 1.4 multiply_subtract_fusion.3
  558.2 1.6 multiply_subtract_fusion.2
  559.8 1.6 multiply_subtract_fusion.1
  561.4 1.6 multiply_subtract_fusion
  563.0 115.0 %all-reduce.13.cloned.1.call-done = (bf16[8,384,384]{2,1,0:T(8,128)(2,1)}, bf16[8,384,384]{2,1,0:T(8,128)(2,1)}) async-done(((bf16[8,384,384]{2,1,0:T(8,128)(2,1)}, bf16[8,384,384]{2,1,0:T(8,128)(2,1)}), (bf16[8,384,384]{2,1,0:T(8,128)(2,1)}, bf16[8,384,384]{2,1,0:T(8,128)(2,1)})) %all-reduce.13.cloned.1.call-update) | async-done | bytes 4718608 | tf_op jit(solution)/shard_map/psum | solution.py:114
  678.0 5.8 convert_add_fusion
  683.8 0.2 copy-done.2
  683.9 1.3 fusion.13
  685.3 2.5 fusion.14
  687.8 33.2 %psum.71 = f32[2,384]{1,0:T(2,128)S(1)} all-reduce(f32[2,384]{1,0:T(2,128)S(1)} %pad_maximum_fusion.3), channel_id=1, replica_groups=mesh['dp'=16,'mp'=2] {'dp'}, use_global_device_ids=true, to_apply=%region_21.22 | all-reduce | flops 768 | bytes 6144 | tf_op jit(solution)/shard_map/psum | solution.py:169
  720.9 8.3 %add_add_fusion.2 = f32[8,384,384]{2,1,0:T(8,128)} fusion(f32[8,384]{1,0:T(8,128)S(1)} %negate_multiply_fusion.1, f32[8,384]{1,0:T(8,128)S(1)} %multiply_multiply_fusion.9, f32[8,384,384]{2,1,0:T(8,128)} %param.18, f32[8,384]{1,0:T(8,128)S(1)} %broadcast_multiply_fusion.1, f32[8,384]{1,0:T(8,128)S(1)} %fusion.63, f32[384]{0:T(512)S(1)} %get-tuple-element.29, ...), kind=kLoop, calls=%fused_computation.41 | loop fusion | flops 12976128 | bytes 21296640 | tf_op jit(solution)/shard_map/add | solution.py:166
  729.2 0.7 multiply_subtract_fusion.4
  (93 shorter events, 0.3 us)
Async XLA Ops:
  7.2 213.8 %all-reduce.7.cloned.1.call-start = ((), (), s32[]{:S(2)}) async-start(), calls=%async_computation | async-start | bytes 9437184 | tf_op jit(solution)/shard_map/psum | solution.py:109
  32.5 6.1 copy-start.7
  38.6 45.3 %copy-start.11 = (f32[8,384]{1,0:T(8,128)}, f32[8,384]{1,0:T(8,128)S(1)}, u32[]{:S(2)}) copy-start(f32[8,384]{1,0:T(8,128)S(1)} %multiply_reduce_fusion.4) | copy-start | bytes 36868
  77.5 16.0 %copy-start.5 = (bf16[3,384,192]{1,2,0:T(8,128)(2,1)}, bf16[3,384,192]{1,2,0:T(8,128)(2,1)S(1)}, u32[]{:S(2)}) copy-start(bf16[3,384,192]{1,2,0:T(8,128)(2,1)S(1)} %copy.80) | copy-start | bytes 1327108
  93.5 7.7 %copy-start.20 = (f32[8,3,384]{2,1,0:T(4,128)}, f32[8,3,384]{2,1,0:T(4,128)S(1)}, u32[]{:S(2)}) copy-start(f32[8,3,384]{2,1,0:T(4,128)S(1)} %get-tuple-element.62) | copy-start | bytes 110596
  101.2 3.3 copy-start.9
  101.2 3.3 copy-start.10
  104.4 284.9 %all-reduce.9.cloned.1.call-start = ((), (), s32[]{:S(2)}) async-start(), calls=%async_computation.1 | async-start | bytes 9437184 | tf_op jit(solution)/shard_map/psum | solution.py:128
  225.4 6.2 copy-start
  225.4 28.5 %slice-start.4 = ((s8[4718592]{0:T(1024)(128)(4,1)}), s8[4194304]{0:T(1024)(128)(4,1)S(1)}, s32[]{:S(2)}) async-start(s8[4718592]{0:T(1024)(128)(4,1)} %bitcast.139), calls=%async_computation.8 | async-start | bytes 8388608
  226.3 27.6 %slice-start.5 = ((s8[4718592]{0:T(1024)(128)(4,1)}), s8[524288]{0:T(1024)(128)(4,1)S(1)}, s32[]{:S(2)}) async-start(s8[4718592]{0:T(1024)(128)(4,1)} %bitcast.139), calls=%async_computation.9 | async-start | bytes 1048576
  269.9 7.0 slice-start.2
  270.0 286.8 %all-reduce.11.cloned.1.call-start = ((), (), s32[]{:S(2)}) async-start(), calls=%async_computation.2 | async-start | bytes 7864320 | tf_op jit(solution)/shard_map/psum | solution.py:169
  270.0 7.0 slice-start.3
  389.3 5.1 copy-start.3
  389.3 9.6 %slice-start.6 = ((s8[4718592]{0:T(1024)(128)(4,1)}), s8[4194304]{0:T(1024)(128)(4,1)S(1)}, s32[]{:S(2)}) async-start(s8[4718592]{0:T(1024)(128)(4,1)} %bitcast.141), calls=%async_computation.10 | async-start | bytes 8388608
  394.4 4.5 slice-start.7
  398.9 2.1 copy-start.1
  401.1 1.8 copy-start.21
  424.1 10.3 %copy-start.4 = (bf16[3,8,3,384,64]{3,4,2,0,1:T(8,128)(2,1)S(1)}, bf16[3,8,3,384,64]{3,4,2,0,1:T(8,128)(2,1)}, u32[]{:S(2)}) copy-start(bf16[3,8,3,384,64]{3,4,2,0,1:T(8,128)(2,1)} %convert_bitcast_fusion) | copy-start | bytes 10616836
  446.8 6.6 copy-start.6
  446.9 231.1 %all-reduce.13.cloned.1.call-start = ((), (), s32[]{:S(2)}) async-start(), calls=%async_computation.3 | async-start | bytes 9437184 | tf_op jit(solution)/shard_map/psum | solution.py:114
  446.9 6.6 copy-start.27
  446.9 6.6 copy-start.28
  457.3 99.5 %copy-start.13 = (f32[192,24]{0,1:T(8,128)S(1)}, f32[192,24]{0,1:T(8,128)}, u32[]{:S(2)}) copy-start(f32[192,24]{0,1:T(8,128)} %param.22) | copy-start | bytes 55300
  457.3 99.5 %copy-start.22 = (f32[192,24]{0,1:T(8,128)S(1)}, f32[192,24]{0,1:T(8,128)}, u32[]{:S(2)}) copy-start(f32[192,24]{0,1:T(8,128)} %param.27) | copy-start | bytes 55300
  457.3 99.5 %copy-start.23 = (f32[192,24]{0,1:T(8,128)S(1)}, f32[192,24]{0,1:T(8,128)}, u32[]{:S(2)}) copy-start(f32[192,24]{0,1:T(8,128)} %param.32) | copy-start | bytes 55300
  457.3 100.9 %copy-start.8 = (f32[3,24,192]{2,1,0:T(8,128)S(1)}, f32[3,24,192]{2,1,0:T(8,128)}, u32[]{:S(2)}) copy-start(f32[3,24,192]{2,1,0:T(8,128)} %param.21) | copy-start | bytes 165892
  457.3 100.8 %copy-start.14 = (f32[3,24,192]{2,1,0:T(8,128)S(1)}, f32[3,24,192]{2,1,0:T(8,128)}, u32[]{:S(2)}) copy-start(f32[3,24,192]{2,1,0:T(8,128)} %param.26) | copy-start | bytes 165892
  457.3 100.8 %copy-start.15 = (f32[3,24,192]{2,1,0:T(8,128)S(1)}, f32[3,24,192]{2,1,0:T(8,128)}, u32[]{:S(2)}) copy-start(f32[3,24,192]{2,1,0:T(8,128)} %param.31) | copy-start | bytes 165892
  457.3 102.4 %copy-start.16 = (f32[24,768]{1,0:T(8,128)S(1)}, f32[24,768]{1,0:T(8,128)}, u32[]{:S(2)}) copy-start(f32[24,768]{1,0:T(8,128)} %param.28) | copy-start | bytes 221188
  457.3 102.4 %copy-start.17 = (f32[24,768]{1,0:T(8,128)S(1)}, f32[24,768]{1,0:T(8,128)}, u32[]{:S(2)}) copy-start(f32[24,768]{1,0:T(8,128)} %param.33) | copy-start | bytes 221188
  457.4 104.0 %copy-start.18 = (f32[768,24]{0,1:T(8,128)S(1)}, f32[768,24]{0,1:T(8,128)}, u32[]{:S(2)}) copy-start(f32[768,24]{0,1:T(8,128)} %param.29) | copy-start | bytes 221188
  457.4 104.0 %copy-start.19 = (f32[768,24]{0,1:T(8,128)S(1)}, f32[768,24]{0,1:T(8,128)}, u32[]{:S(2)}) copy-start(f32[768,24]{0,1:T(8,128)} %param.34) | copy-start | bytes 221188
  457.4 226.4 %slice-start = ((s8[4718592]{0:T(1024)(128)(4,1)}), s8[524288]{0:T(1024)(128)(4,1)S(1)}, s32[]{:S(2)}) async-start(s8[4718592]{0:T(1024)(128)(4,1)} %bitcast.135), calls=%async_computation.4 | async-start | bytes 1048576
  678.0 5.8 slice-start.1
  678.0 6.0 copy-start.2
  683.8 1.5 copy-start.12
  720.9 8.3 %copy-start.24 = (f32[2,24]{1,0:T(2,128)S(1)}, f32[2,24]{1,0:T(2,128)}, u32[]{:S(2)}) copy-start(f32[2,24]{1,0:T(2,128)} %param.25) | copy-start | bytes 580
  720.9 8.3 %copy-start.25 = (f32[2,24]{1,0:T(2,128)S(1)}, f32[2,24]{1,0:T(2,128)}, u32[]{:S(2)}) copy-start(f32[2,24]{1,0:T(2,128)} %param.30) | copy-start | bytes 580
  720.9 8.3 %copy-start.26 = (f32[2,24]{1,0:T(2,128)S(1)}, f32[2,24]{1,0:T(2,128)}, u32[]{:S(2)}) copy-start(f32[2,24]{1,0:T(2,128)} %param.35) | copy-start | bytes 580
Sparse Core Ops, SparseCore 0:
  104.5 116.4 all-reduce.6
  270.1 119.2 all-reduce.8
  447.0 109.7 all-reduce.10
  559.7 118.2 all-reduce.12
where the time goes:
time: 746 us; the launch traced here: 737 us
  waiting for transfers between devices  397 us (53%)
  blocking collectives  134 us (18%)
  matrix products  104 us (14%)
  other arithmetic  81 us (11%)
  between operations  14.8 us (2%)
    psum x1, waiting for transfers between devices, shards(): lax.psum(feed_term.astype(jnp.bfloat16), 'mp').astype(jnp.float32)  115 us
    psum x1, waiting for transfers between devices, shards(): grad_normed_two = lax.psum(part_two, 'mp')  106 us
    psum x1, waiting for transfers between devices, shards(): lax.psum((all_grads[0], all_grads[1], all_grads[2], all_grads[3], all_gra...  99.3 us
    psum x1, waiting for transfers between devices, shards(): middle = inputs + lax.psum(branch, 'mp')  76.6 us
    psum x1, blocking collectives, shards(): lax.psum((all_grads[0], all_grads[1], all_grads[2], all_grads[3], all_gra...  33.2 us
    all_gather x1, blocking collectives, shards(): lax.all_gather(norm_vectors.astype(jnp.bfloat16), 'dp', axis=1, tiled=True)  23 us
    convert_element_type x1, other arithmetic, feed_part(): active = jax.nn.gelu(hidden, approximate=False).astype(jnp.bfloat16)  22.3 us
    all_gather x1, blocking collectives, shards(): lax.all_gather(up_weight.astype(jnp.bfloat16), 'dp', axis=0, tiled=True)  20.8 us
  transfers between devices with their start and end apart: 4, of which 4 were waited for; matrix products, arithmetic and copies ran while one was open for 4% of the time, Pallas kernels for 0%

commit v1 on v0

v1 whole, which is shorter than its diff:
```python
import functools
import types

import jax
import jax.numpy as jnp
from jax import lax
from jax.experimental import pallas as pl
from jax.experimental.pallas import tpu as pltpu
from jax.sharding import PartitionSpec as P

MESH = pl.DeviceIdType.MESH
bf = jnp.bfloat16
f32 = jnp.float32
S = 384
D = 384
NN=(((1,),(0,)),((),())); NT=(((1,),(1,)),((),())); TN=(((0,),(0,)),((),()))
def dot(a,b,dn=NN): return lax.dot_general(a,b,dn,preferred_element_type=f32)

def ln_stats(x):
    c = x - jnp.mean(x,axis=-1,keepdims=True)
    r = lax.rsqrt(jnp.mean(c*c,axis=-1,keepdims=True)+1e-6)
    return c*r, r

def gelu_parts(u):
    z = jnp.abs(u)*0.7071067811865476
    t = 1.0/(1.0+0.3275911*z)
    poly = t*(0.127414796 + t*(-0.142248368 + t*(0.7107068705 + t*(-0.7265760135 + t*0.5307027145))))
    E = jnp.exp(u*u*-0.5)
    h = poly*E
    phi = jnp.where(u>=0, 1.0-h, h)
    return phi, E*0.3989422804014327

def stack2(t, lo):
    z=jnp.zeros_like(t)
    return jnp.concatenate([jnp.where(lo,t,z),jnp.where(lo,z,t)],axis=0)

def unstackT(t):
    return jnp.concatenate([t[:64,:S],t[64:,S:]],axis=0).T

def a1(img, R, count):
    xh,_ = ln_stats(R.x[img])
    h1=(xh*R.g1).astype(bf)
    R.h1[img]=h1
    for b in range(3):
        for m in range(3):
            c=m*384+128*b
            R.qkv[img,:,c:c+128]=dot(h1,R.wqkv[:,c:c+128]).astype(bf)
    lo=lax.broadcasted_iota(jnp.int32,(S,128),1)<64
    for b in range(3):
        q=R.qkv[img,:,128*b:128*b+128]*jnp.asarray(0.125,bf)
        k=R.qkv[img,:,384+128*b:512+128*b]
        v=R.qkv[img,:,768+128*b:896+128*b]
        q2=stack2(q,lo)
        s=dot(k,q2,NT)
        key=lax.broadcasted_iota(jnp.int32,(128,2*S),0)
        s=jnp.concatenate([s[:256],jnp.where(key<count,s[256:],-1e30)],axis=0)
        mx=jnp.max(s,axis=0,keepdims=True)
        e=jnp.exp(s-mx)
        p=e*(1.0/jnp.sum(e,axis=0,keepdims=True))
        R.p[img,b]=p
        oT=dot(v,p.astype(bf),TN)
        R.o[img,:,128*b:128*b+128]=unstackT(oT).astype(bf)

CH=512
def a2(img, R):
    o=R.o[img]; x=R.x[img]; g=R.g[img]
    y1=x+dot(o,R.wo[...],NT)
    xh2,r2=ln_stats(y1)
    h2=(xh2*R.g2).astype(bf)
    dl=g.astype(bf)
    bo=y1; dh2=jnp.zeros((S,D),f32)
    for c0 in range(0,1536,CH):
        c=slice(c0,c0+CH)
        u=dot(h2,R.wu[:,c])
        da=dot(dl,R.wd[:,c])
        phi,ph=gelu_parts(u)
        a=(u*phi).astype(bf)
        du=(da*(phi+u*ph)).astype(bf)
        bo=bo+dot(a,R.wd[:,c],NT)
        dh2=dh2+dot(du,R.wu[:,c],NT)
        R.Gu[:,c]=R.Gu[:,c]+dot(h2,du,TN)
        R.Gd[:,c]=R.Gd[:,c]+dot(dl,a,TN)
    R.bo[img]=bo.astype(R.bo.dtype)
    e=dh2*R.g2
    m1=jnp.mean(e,axis=-1,keepdims=True)
    m2=jnp.mean(e*xh2,axis=-1,keepdims=True)
    dy=g+r2*(e-m1-xh2*m2)
    R.dy[img]=dy
    R.gn[1:2,:]=R.gn[1:2,:]+jnp.sum(dh2*xh2,axis=0,keepdims=True)
    R.Go[...]=R.Go[...]+dot(dy.astype(bf),o,TN)

def cc(img, R):
    dy=R.dy[img]
    dm=dy.astype(bf)
    h1=R.h1[img]
    lo=lax.broadcasted_iota(jnp.int32,(S,128),1)<64
    dh1=jnp.zeros((S,D),f32)
    for b in range(3):
        sl=slice(128*b,128*b+128)
        do=dot(dm,R.wo[:,sl]).astype(bf)
        do2=stack2(do,lo)
        q2=stack2(R.qkv[img,:,sl]*jnp.asarray(0.125,bf),lo)
        k=R.qkv[img,:,384+128*b:512+128*b]
        v=R.qkv[img,:,768+128*b:896+128*b]
        p=R.p[img,b]
        dv=dot(p.astype(bf),do2).astype(bf)
        dp=dot(v,do2,NT)
        inner=jnp.sum(p*dp,axis=0,keepdims=True)
        ds=(p*(dp-inner)).astype(bf)
        dk=dot(ds,q2).astype(bf)
        dq=(unstackT(dot(k,ds,TN))*0.125).astype(bf)
        R.dqkv[:,sl]=dq; R.dqkv[:,384+128*b:512+128*b]=dk; R.dqkv[:,768+128*b:896+128*b]=dv
    dqkv=R.dqkv[...]
    R.Gqkv[...]=R.Gqkv[...]+dot(h1,dqkv,TN)
    dh1=dot(dqkv,R.wqkv[...],NT)
    xh1,r1=ln_stats(R.x[img])
    e=dh1*R.g1
    m1=jnp.mean(e,axis=-1,keepdims=True)
    m2=jnp.mean(e*xh1,axis=-1,keepdims=True)
    ig=dy+r1*(e-m1-xh1*m2)
    R.ig[img]=ig.astype(R.ig.dtype)
    R.gn[0:1,:]=R.gn[0:1,:]+jnp.sum(dh1*xh1,axis=0,keepdims=True)


STEP = 5
EPS_ADAM = 1e-08
BETA_FIRST = 0.5
BETA_SECOND = 0.5
DECAY_MATRIX = 0.01
RATE_QKV = 0.05
RATE_OUT = 0.2
RATE_UP = 0.05
RATE_DOWN = 0.03
RATE_NORM = 0.3


class Plan:
    def __init__(self, dp, mp, rows, images):
        assert mp == 2 and dp & (dp - 1) == 0
        self.dp, self.mp, self.rows = dp, mp, rows
        self.bits = dp.bit_length() - 1
        self.stages = self.bits + 1
        self.slots = dp * mp
        self.folded = -(-2 * rows // 16) * 16
        self.images = images
        self.here = images // mp
        high = [("dp", b) for b in range(self.bits - 1, 1, -1)]
        x, y, core = ("mp", 0), ("dp", 1), ("dp", 0)
        self.gather = [
            (0, 2, high + [x, y, core]),
            (2, 1, high + [y, x, core]),
            (3, 2, high + [x, y, core]),
            (5, 4, high + [y, x, core]),
        ]
        self.scatter = [
            (0, 2, high + [x, y, core]),
            (2, 1, high + [y, x, core]),
            (3, 2, high + [x, y, core]),
            (5, 4, high + [y, x, core]),
        ]


def slot_of(order, i, j):
    total = 0
    for t, (axis, b) in enumerate(order):
        bit = j if axis == "mp" else (i // 2**b) % 2
        total = total + bit * 2**t
    return total


class Place:
    def __init__(self):
        self.i = lax.axis_index("dp")
        self.j = lax.axis_index("mp")

    def bit(self, axis_bit):
        axis, b = axis_bit
        return self.j if axis == "mp" else lax.rem(self.i // 2**b, 2)

    def partner(self, axis_bit):
        axis, b = axis_bit
        if axis == "mp":
            return {"mp": 1 - self.j}
        return {"dp": self.i + 2**b - 2 ** (b + 1) * self.bit(axis_bit)}

    def slot(self, order):
        total = 0
        for t, axis_bit in enumerate(order):
            total = total + self.bit(axis_bit) * 2**t
        return total


def remote(src, dst, send, recv, where):
    return pltpu.make_async_remote_copy(
        src_ref=src, dst_ref=dst, send_sem=send, recv_sem=recv, device_id=where, device_id_type=MESH
    )


class Gather:
    def __init__(self, place, order, buf, send, recv):
        self.place, self.order, self.buf = place, order, buf
        self.send, self.recv = send, recv
        self.slot = place.slot(order)

    def copy(self, t):
        size = 2**t
        start = self.slot - lax.rem(self.slot, size)
        part = self.buf.at[pl.ds(start, size)]
        return remote(
            part, part, self.send.at[t], self.recv.at[t], self.place.partner(self.order[t])
        )

    def start(self, t):
        self.copy(t).start()

    def wait(self, t):
        self.copy(t).wait_recv()

    def finish(self):
        for t in range(len(self.order)):
            self.copy(t).wait_send()


class Scatter:
    def __init__(self, place, order, total, out, came, send, recv):
        self.place, self.order, self.total = place, order, total
        self.out, self.came, self.send, self.recv = out, came, send, recv
        self.top = len(order) - 1
        self.own = place.slot(order[:-1])

    def copy(self, t):
        size = 2**t
        here = pl.ds(size, size)
        return remote(
            self.out.at[here],
            self.came.at[here],
            self.send.at[t],
            self.recv.at[t],
            self.place.partner(self.order[t]),
        )

    def kept(self, t):
        return self.own - lax.rem(self.own, 2**t)

    def start(self, t):
        if t < self.top:
            size = 2**t
            base = self.own - lax.rem(self.own, 2 * size)
            away = base + (1 - self.place.bit(self.order[t])) * size
            self.out[pl.ds(size, size)] = self.total[pl.ds(away, size)].astype(bf)
        self.copy(t).start()

    def add(self, t):
        size = 2**t
        self.copy(t).wait_recv()
        keep = 0 if t == self.top else self.kept(t)
        self.total[pl.ds(keep, size)] = self.total[pl.ds(keep, size)] + self.came[
            pl.ds(size, size)
        ].astype(f32)

    def finish(self):
        for t in range(self.top + 1):
            self.copy(t).wait_send()


def low_half(rows):
    return lax.broadcasted_iota(jnp.int32, (rows, 128), 1) < 64


def unpack(plan, groups, bufs, R, which):
    rows = plan.rows
    step = 16
    while step % rows and (step // 16) < 64:
        step += 16
    per = max(step // rows, 1)
    if (per * rows) % 16:
        raise ValueError("rows")
    first, last = (0, 3) if which == "A" else (3, 9)
    for m in range(plan.dp // per):
        tops, bottoms = [[], []], [[], []]
        for j in range(2):
            for f in range(first, last):
                g = next(n for n, e in enumerate(groups) if e[0] <= f < e[0] + e[1])
                lane = 128 * (f - groups[g][0])
                parts = [
                    bufs[g][slot_of(groups[g][2], m * per + n, j), :, lane : lane + 128].astype(f32)
                    for n in range(per)
                ]
                tops[j].append(jnp.concatenate([q[:rows] for q in parts], axis=0))
                bottoms[j].append(jnp.concatenate([q[rows : 2 * rows] for q in parts], axis=0))
        c0, c1 = tops[0] + bottoms[0], tops[1] + bottoms[1]
        size = per * rows
        lo = low_half(size)
        at = slice(m * size, (m + 1) * size)

        def put(ref, block, value):
            ref[at, 128 * block : 128 * block + 128] = value.astype(bf)

        if which == "A":
            for n in range(3):
                put(R.wqkv, 3 * n, c0[n])
                put(R.wqkv, 3 * n + 1, jnp.where(lo, c0[3 + n], c1[3 + n]))
                put(R.wqkv, 3 * n + 2, c1[n])
            put(R.wu, 10, jnp.where(lo, c1[3], c0[3]))
            put(R.wu, 11, jnp.where(lo, c1[4], c0[4]))
            put(R.wd, 10, jnp.where(lo, c1[5], c0[5]))
        else:
            put(R.wo, 0, c0[0])
            put(R.wo, 1, jnp.where(lo, c0[1], c1[1]))
            put(R.wo, 2, c1[0])
            put(R.wd, 11, jnp.where(lo, c1[1], c0[1]))
            for n in range(5):
                put(R.wu, n, c0[2 + n])
                put(R.wu, 5 + n, c1[2 + n])
                put(R.wd, n, c0[7 + n])
                put(R.wd, 5 + n, c1[7 + n])


def pack(plan, groups, scatters, R, core, which):
    rows = plan.rows
    lo = low_half(2 * rows)
    first, last = (0, 3) if which == "A" else (3, 9)
    for r in range(plan.dp // 2):
        at = slice(2 * r * rows, 2 * (r + 1) * rows)

        def get(ref, block):
            return ref[at, 128 * block : 128 * block + 128]

        def piece(j, n):
            if which == "A":
                if n < 3:
                    return get(R.Gqkv, 3 * n + 2 * j)
                own = get(R.Gqkv, 3 * (n - 3) + 1)
                fill = get(R.Gu, 7 + n) if n < 5 else get(R.Gd, 10)
            elif n == 0:
                return get(R.Go, 2 * j)
            elif n == 1:
                own, fill = get(R.Go, 1), get(R.Gd, 11)
            elif n < 7:
                return get(R.Gu, n - 2 + 5 * j)
            else:
                return get(R.Gd, n - 7 + 5 * j)
            return jnp.where(lo, own, fill) if j == 0 else jnp.where(lo, fill, own)

        for j in range(2):
            for f in range(first, last):
                g = next(n for n, e in enumerate(groups) if e[0] <= f < e[0] + e[1])
                lane = 128 * (f - groups[g][0])
                n = f - first
                top, bottom = piece(j, n), piece(j, n + last - first)
                even = jnp.concatenate([top[:rows], bottom[:rows]], axis=0)
                odd = jnp.concatenate([top[rows:], bottom[rows:]], axis=0)
                if plan.folded > 2 * rows:
                    none = jnp.zeros((plan.folded - 2 * rows, 128), f32)
                    even = jnp.concatenate([even, none], axis=0)
                    odd = jnp.concatenate([odd, none], axis=0)
                slot = slot_of(groups[g][2][:-1], 2 * r, j)
                half = plan.slots // 2
                scatters[g].out[half + slot, :, lane : lane + 128] = jnp.where(
                    core == 0, odd, even
                ).astype(bf)
                scatters[g].total[slot, :, lane : lane + 128] = jnp.where(core == 0, even, odd)


def layer_kernel(plan, *refs):
    it = iter(refs)
    take = lambda n: [next(it) for _ in range(n)]
    counts, inputs, out_grad, packed, gpos = take(5)
    bo_out, ig_out, grads_out, gn_out = take(4)
    x, g, h1, qkv, p, o, dy, dqkv = take(8)
    wqkv, wo, wu, wd, Gqkv, Go, Gu, Gd, gn = take(9)
    bo, ig = take(2)
    ng = len(plan.gather)
    gbufs = take(ng)
    g_send, g_recv = take(2)
    ns = len(plan.scatter)
    totals, outs, cames = take(ns), take(ns), take(ns)
    s_send, s_recv = take(2)
    gains, gains_in, gains_send, gains_recv = take(4)
    sums, sums_in, sums_send, sums_recv = take(4)
    load_sem, store_sem, x_send, x_recv = take(4)

    place = Place()
    j = place.j
    every = [("dp", b) for b in range(plan.bits)] + [("mp", 0)]
    here = plan.here

    loads = []
    for n in range(here):
        for k, (src, dst) in enumerate(((inputs, x), (out_grad, g))):
            loads.append(
                pltpu.make_async_copy(src.at[j * here + n], dst.at[n], load_sem.at[k, n])
            )
    for c in loads:
        c.start()

    barrier = pltpu.get_barrier_semaphore()
    for axis_bit in every:
        pl.semaphore_signal(
            barrier, inc=1, device_id=place.partner(axis_bit), device_id_type=MESH
        )

    gathers = [
        Gather(place, order, gbufs[n], g_send.at[n], g_recv.at[n])
        for n, (_, _, order) in enumerate(plan.gather)
    ]
    for n, (f, size, _) in enumerate(plan.gather):
        gbufs[n][gathers[n].slot] = packed[:, 128 * f : 128 * (f + size)]
    gains[0] = gpos[...]
    scatters = [
        Scatter(place, order, totals[n], outs[n], cames[n], s_send.at[n], s_recv.at[n])
        for n, (_, _, order) in enumerate(plan.scatter)
    ]
    first = [n for n in range(ng) if plan.gather[n][0] < 3]
    second = [n for n in range(ng) if plan.gather[n][0] >= 3]
    early = [n for n in range(ns) if plan.scatter[n][0] >= 3]
    late = [n for n in range(ns) if plan.scatter[n][0] < 3]
    top = plan.stages - 1

    gain_order = [("dp", b) for b in range(plan.bits - 1, -1, -1)]

    def gain_copy(t):
        return remote(
            gains.at[t],
            gains_in.at[t],
            gains_send.at[t],
            gains_recv.at[t],
            place.partner(gain_order[t]),
        )

    sum_order = gain_order + [("mp", 0)]

    def sum_copy(t):
        return remote(
            sums.at[t], sums_in.at[t], sums_send.at[t], sums_recv.at[t], place.partner(sum_order[t])
        )

    pl.semaphore_wait(barrier, len(every))

    for t in range(plan.stages):
        for n in first:
            if t:
                gathers[n].wait(t - 1)
            gathers[n].start(t)
        if t < plan.bits:
            if t:
                gain_copy(t - 1).wait_recv()
                gains[t] = gains[t - 1] + gains_in[t - 1]
            gain_copy(t).start()
        if t < top - 1:
            for n in second:
                if t:
                    gathers[n].wait(t - 1)
                gathers[n].start(t)
        if t == 0:
            for ref in (Gqkv, Go, Gu, Gd, gn):
                ref[...] = jnp.zeros_like(ref)
    gain_copy(plan.bits - 1).wait_recv()
    gains[plan.bits] = gains[plan.bits - 1] + gains_in[plan.bits - 1]
    for n in first:
        gathers[n].wait(top)
    R = types.SimpleNamespace(
        x=x, g=g, h1=h1, qkv=qkv, p=p, o=o, dy=dy, dqkv=dqkv, wqkv=wqkv, wo=wo, wu=wu, wd=wd,
        Gqkv=Gqkv, Go=Go, Gu=Gu, Gd=Gd, gn=gn, bo=bo, ig=ig,
    )
    unpack(plan, plan.gather, gbufs, R, "A")
    R.g1 = gains[plan.bits, 0:1, :]
    R.g2 = gains[plan.bits, 1:2, :]

    for n in second:
        gathers[n].wait(top - 2)
        gathers[n].start(top - 1)
    for c in loads:
        c.wait()

    def attend(n, carry):
        a1(n, R, counts[j * here + n])

        @pl.when(n == (here - 1) // 2)
        def _():
            for k in second:
                gathers[k].wait(top - 1)
                gathers[k].start(top)

        return carry

    lax.fori_loop(0, here, attend, 0)
    for n in second:
        gathers[n].wait(top)
    unpack(plan, plan.gather, gbufs, R, "B")

    def swap(n, k):
        ref, out = ((bo, bo_out), (ig, ig_out))[k]
        return (
            pltpu.make_async_copy(ref.at[n], out.at[j * here + n], store_sem.at[k, n]),
            remote(
                ref.at[n], out.at[j * here + n], x_send.at[k, n], x_recv.at[k, n], {"mp": 1 - j}
            ),
        )

    def feed(n, carry):
        a2(n, R)
        for c in swap(n, 0):
            c.start()
        return carry

    lax.fori_loop(0, here, feed, 0)

    core = place.bit(("dp", 0))
    pack(plan, plan.scatter, scatters, R, core, "B")
    for n in early:
        scatters[n].start(top)

    marks = [top - 1 - ((top + 1) * n) // here for n in range(here)]

    def back(n, carry):
        cc(n, R)
        for c in swap(n, 1):
            c.start()
        t_done = top
        for image in range(here - 1):
            stages = list(range(t_done, max(t_done - 2, 0) if image else t_done - 1, -1))[:2]
            stages = stages[:1] if image < here - 2 else stages

            @pl.when(n == image)
            def _(stages=stages):
                for t in stages:
                    for k in early:
                        scatters[k].add(t)
                        if t:
                            scatters[k].start(t - 1)

            t_done = stages[-1] - 1 if stages else t_done
        back.t_done = t_done
        return carry

    lax.fori_loop(0, here, back, 0)

    pack(plan, plan.scatter, scatters, R, core, "A")
    sums[0] = gn[...]
    for n in late:
        scatters[n].start(top)
    sum_copy(0).start()
    t_early = back.t_done
    for step in range(top + 1):
        t = top - step
        for n in late:
            scatters[n].add(t)
            if t:
                scatters[n].start(t - 1)
        sum_copy(step).wait_recv()
        sums[step + 1] = sums[step] + sums_in[step]
        if step < top:
            sum_copy(step + 1).start()
        if t_early >= 0:
            for n in early:
                scatters[n].add(t_early)
                if t_early:
                    scatters[n].start(t_early - 1)
            t_early -= 1
    for n, (f, size, _) in enumerate(plan.scatter):
        grads_out[:, 128 * f : 128 * (f + size)] = totals[n][scatters[n].own]
    gn_out[...] = sums[plan.stages]

    for c in gathers + scatters:
        c.finish()
    for t in range(plan.bits):
        gain_copy(t).wait_send()
    for t in range(plan.stages):
        sum_copy(t).wait_send()
    for n in range(here):
        for k in range(2):
            own, away = swap(n, k)
            own.wait()
            away.wait()


def run_layer(plan, counts, inputs, out_grad, packed, gpos):
    here, slots, folded = plan.here, plan.slots, plan.folded
    vmem = pl.BlockSpec(memory_space=pltpu.VMEM)
    hbm = pl.BlockSpec(memory_space=pl.ANY)
    dma = pltpu.SemaphoreType.DMA
    out = jax.ShapeDtypeStruct
    ng, ns = len(plan.gather), len(plan.scatter)
    lanes_g = [128 * e[1] for e in plan.gather]
    lanes_s = [128 * e[1] for e in plan.scatter]
    scratch = [
        pltpu.VMEM((here, S, D), f32),
        pltpu.VMEM((here, S, D), f32),
        pltpu.VMEM((here, S, D), bf),
        pltpu.VMEM((here, S, 3 * D), bf),
        pltpu.VMEM((here, 3, S, 2 * S), f32),
        pltpu.VMEM((here, S, D), bf),
        pltpu.VMEM((here, S, D), f32),
        pltpu.VMEM((S, 3 * D), bf),
        pltpu.VMEM((D, 3 * D), bf),
        pltpu.VMEM((D, D), bf),
        pltpu.VMEM((D, 4 * D), bf),
        pltpu.VMEM((D, 4 * D), bf),
        pltpu.VMEM((D, 3 * D), f32),
        pltpu.VMEM((D, D), f32),
        pltpu.VMEM((D, 4 * D), f32),
        pltpu.VMEM((D, 4 * D), f32),
        pltpu.VMEM((8, D), f32),
        pltpu.VMEM((here, S, D), bf),
        pltpu.VMEM((here, S, D), bf),
    ]
    scratch += [pltpu.VMEM((slots, folded, n), bf) for n in lanes_g]
    scratch += [dma((ng, plan.stages)), dma((ng, plan.stages))]
    scratch += [pltpu.VMEM((slots // 2, folded, n), f32) for n in lanes_s]
    scratch += [pltpu.VMEM((slots, folded, n), bf) for n in lanes_s]
    scratch += [pltpu.VMEM((slots, folded, n), bf) for n in lanes_s]
    scratch += [dma((ns, plan.stages)), dma((ns, plan.stages))]
    scratch += [
        pltpu.VMEM((plan.bits + 1, 8, D), f32),
        pltpu.VMEM((plan.bits, 8, D), f32),
        dma((plan.bits,)),
        dma((plan.bits,)),
        pltpu.VMEM((plan.stages + 1, 8, D), f32),
        pltpu.VMEM((plan.stages, 8, D), f32),
        dma((plan.stages,)),
        dma((plan.stages,)),
        dma((2, here)),
        dma((2, here)),
        dma((2, here)),
        dma((2, here)),
    ]
    return pl.pallas_call(
        functools.partial(layer_kernel, plan),
        out_shape=[
            out(inputs.shape, bf),
            out(inputs.shape, bf),
            out((folded, 9 * 128), f32),
            out((8, D), f32),
        ],
        in_specs=[pl.BlockSpec(memory_space=pltpu.SMEM), hbm, hbm, vmem, vmem],
        out_specs=[hbm, hbm, vmem, vmem],
        scratch_shapes=scratch,
        compiler_params=pltpu.CompilerParams(
            collective_id=0, has_side_effects=True, vmem_limit_bytes=63 << 20
        ),
        name="layer",
    )(counts, inputs, out_grad, packed, gpos)


def fold(a, folded):
    half = a.shape[1] // 2
    out = jnp.concatenate([a[:, :half], a[:, half:]], axis=0)
    return jnp.pad(out, ((0, folded - out.shape[0]), (0, 0)))


def adamw_update(weight, gradient, first_moment, second_moment, step_rate, decay_rate):
    first_next = BETA_FIRST * first_moment + (1.0 - BETA_FIRST) * gradient
    second_next = BETA_SECOND * second_moment + (1.0 - BETA_SECOND) * gradient * gradient
    first_fixed = first_next / (1.0 - BETA_FIRST**STEP)
    second_fixed = second_next / (1.0 - BETA_SECOND**STEP)
    weight_next = weight - step_rate * (
        first_fixed / (jnp.sqrt(second_fixed) + EPS_ADAM) + decay_rate * weight
    )
    return (weight_next, first_next, second_next)


def shards(
    dp, mp, inputs, out_grad, counts,
    qkv_weight, out_weight, up_weight, down_weight, norm_vectors,
    qkv_first, out_first, up_first, down_first, norm_first,
    qkv_second, out_second, up_second, down_second, norm_second,
):
    rows = up_weight.shape[0]
    plan = Plan(dp, mp, rows, inputs.shape[0])
    i, j = lax.axis_index("dp"), lax.axis_index("mp")
    oT, dT, u = out_weight.T, down_weight.T, up_weight
    q, k, v = qkv_weight[0], qkv_weight[1], qkv_weight[2]

    def mix(own, fill):
        return jnp.where(
            j == 0,
            jnp.concatenate([own, fill], axis=1),
            jnp.concatenate([fill, own], axis=1),
        )

    part_a = jnp.concatenate(
        [
            q[:, :128], k[:, :128], v[:, :128],
            mix(q[:, 128:], u[:, 640:704]),
            mix(k[:, 128:], u[:, 704:]),
            mix(v[:, 128:], dT[:, 640:704]),
        ],
        axis=1,
    )
    part_b = jnp.concatenate(
        [oT[:, :128], mix(oT[:, 128:], dT[:, 704:]), u[:, :640], dT[:, :640]], axis=1
    )
    packed = jnp.concatenate(
        [fold(part_a, plan.folded), fold(part_b, plan.folded)], axis=1
    ).astype(bf)
    rounded = lax.reduce_precision(norm_vectors, 8, 7)
    gpos = lax.dynamic_update_slice(jnp.zeros((8, D), f32), rounded, (0, i * rows))

    bo, ig, grads, sums = run_layer(plan, counts, inputs, out_grad, packed, gpos)

    ga = jnp.concatenate([grads[:rows, :384], grads[rows : 2 * rows, :384]], axis=1)
    gb = jnp.concatenate([grads[:rows, 384:], grads[rows : 2 * rows, 384:]], axis=1)

    def split(block):
        left, right = block[:, :64], block[:, 64:]
        return jnp.where(j == 0, left, right), jnp.where(j == 0, right, left)

    mixed = [split(ga[:, 384 + 128 * n : 512 + 128 * n]) for n in range(3)]
    mixed_o = split(gb[:, 128:256])
    qkv_grad = jnp.stack(
        [jnp.concatenate([ga[:, 128 * n : 128 * n + 128], mixed[n][0]], axis=1) for n in range(3)]
    )
    out_grad_w = jnp.concatenate([gb[:, :128], mixed_o[0]], axis=1).T
    up_grad = jnp.concatenate([gb[:, 256:896], mixed[0][1], mixed[1][1]], axis=1)
    down_grad = jnp.concatenate([gb[:, 896:], mixed[2][1], mixed_o[1]], axis=1).T
    norm_grad = lax.dynamic_slice(sums, (0, i * rows), (2, rows))

    new = [
        adamw_update(qkv_weight, qkv_grad, qkv_first, qkv_second, RATE_QKV, DECAY_MATRIX),
        adamw_update(out_weight, out_grad_w, out_first, out_second, RATE_OUT, DECAY_MATRIX),
        adamw_update(up_weight, up_grad, up_first, up_second, RATE_UP, DECAY_MATRIX),
        adamw_update(down_weight, down_grad, down_first, down_second, RATE_DOWN, DECAY_MATRIX),
        adamw_update(norm_vectors, norm_grad, norm_first, norm_second, RATE_NORM, 0.0),
    ]
    return (
        bo.astype(f32),
        ig.astype(f32),
        *[e[0] for e in new],
        *[e[1] for e in new],
        *[e[2] for e in new],
        qkv_grad, out_grad_w, up_grad, down_grad, norm_grad,
    )


def solution(mesh):
    stored = (
        P(None, "dp", "mp"),
        P("mp", "dp"),
        P("dp", "mp"),
        P("mp", "dp"),
        P(None, "dp"),
    )
    images = P("dp", None, None)
    return jax.shard_map(
        functools.partial(shards, mesh.shape["dp"], mesh.shape["mp"]),
        mesh=mesh,
        in_specs=(images, images, P("dp")) + stored * 3,
        out_specs=(images, images) + stored * 4,
        check_vma=False,
    )
```

time: 746 us -> 154 us (0.21); the launches traced: 737 us -> 154 us
  waiting for transfers between devices: 397 us -> 0 us
  blocking collectives: 134 us -> 0 us
  Pallas kernels: 0 us -> 133 us
  matrix products: 104 us -> 0 us
  other arithmetic: 81 us -> 12.7 us
  between operations: 14.8 us -> 0.94 us
    psum x4 -> x0, waiting for transfers between devices: 397 us -> none  [the longest x1 115 us: shards(): lax.psum(feed_term.astype(jnp.bfloat16), 'mp').astype(jnp.float32)]
    pallas_call x0 -> x1, Pallas kernels: none -> 133 us  [run_layer(): pl.pallas_call(functools.partial(layer_kernel, plan), out_shape=[out(inpu...]
    all_gather x5 -> x0, blocking collectives: 101 us -> none  [the longest x1 23 us: shards(): lax.all_gather(norm_vectors.astype(jnp.bfloat16), 'dp', axis=1, tiled=True)]
    dot_general x17 -> x0, matrix products: 94.9 us -> none  [the longest x1 13 us: shards(): jnp.einsum('bhqe,bhke->bhqk', grad_mixed, value_rows, preferred_element_t...]
    psum x1 -> x0, blocking collectives: 33.2 us -> none  [shards(): lax.psum((all_grads[0], all_grads[1], all_grads[2], all_grads[3], all_gra...]
    convert_element_type x8 -> x2, other arithmetic: 34 us -> 6.83 us  [the longest x1 4.32 us: shards(): bo.astype(f32)]
    reduce_sum x8 -> x0, other arithmetic: 24.5 us -> none  [the longest x3 8.68 us: layer_norm(): return shifted * lax.rsqrt(spread + EPS_NORM) * gain_row]
    add x3 -> x0, other arithmetic: 14.7 us -> none  [the longest x1 8.28 us: shards(): input_grad = grad_middle + grad_input_norm]
  transfers between devices with their start and end apart: 4 -> 0, of which waited for: 4 -> 0; matrix products, arithmetic and copies ran while one was open for 4% -> 0% of each run, Pallas kernels for 0% -> 0%
where the time goes in v1:
time: 154 us
  Pallas kernels  133 us (86%)
  other arithmetic  12.7 us (8%)
  local copies, waits for them, and re-layouts  6.55 us (4%)
    pallas_call x1, Pallas kernels, run_layer(): pl.pallas_call(functools.partial(layer_kernel, plan), out_shape=[out(inpu...  133 us
    convert_element_type x1, other arithmetic, shards(): bo.astype(f32)  4.32 us
    sub x5, other arithmetic, adamw_update(): weight - step_rate * (first_fixed / (jnp.sqrt(second_fixed) + EPS_ADAM) +...  4.31 us

profile of v1, /device:TPU:0, one launch (start us, length us, event | category | flops | bytes accessed | tf_op | source)
XLA Modules:
  0.0 153.5 jit_solution(7677349524890593432)
XLA Ops:
  0.7 0.8 slice.212
  1.5 0.8 slice.213
  2.3 0.9 fusion.26
  3.2 0.8 slice_bitcast_fusion.2
  4.0 0.7 slice.184
  4.7 0.1 fusion.14
  4.8 0.7 slice.214
  5.5 0.9 fusion.25
  6.3 0.1 fusion.12
  6.4 0.7 fusion.5.refs_3_
  7.1 0.7 reduce_precision.3
  7.8 0.2 dynamic_update_slice.3.refs_4_
  8.0 0.0 copy-start.12
  8.0 0.6 copy-done.12
  8.6 133.3 %layer.1 = (bf16[8,384,384]{2,1,0:T(8,128)(2,1)}, bf16[8,384,384]{2,1,0:T(8,128)(2,1)}, f32[48,1152]{1,0:T(8,128)}, f32[8,384]{1,0:T(8,128)}) custom-call(s32[8]{0:T(128)} %refs_0_.1, f32[8,384,384]{2,1,0:T(8,128)} %refs_1_.1, f32[8,384,384]{2,1,0:T(8,128)} %refs_2_.1, bf16[48,1152]{1,0:T(8,128)(2,1)} %fusion.5.refs_3_, f32[8,384]{1,0:T(8,128)} %copy-done.12), custom_call_target="tpu_custom_call" | custom-call | tf_op jit(solution)/shard_map/layer/pallas_call | solution.py:628
  141.9 0.0 copy-start
  141.9 4.3 %convert_element_type.7 = f32[8,384,384]{2,1,0:T(8,128)} convert(bf16[8,384,384]{2,1,0:T(8,128)(2,1)} %get-tuple-element.26) | non-fusion elementwise | flops 1179648 | bytes 7077888 | tf_op jit(solution)/shard_map/convert_element_type | solution.py:727
  146.3 0.0 copy-start.1
  146.3 0.0 copy-start.4
  146.3 0.0 copy-start.5
  146.3 0.0 copy-start.6
  146.3 0.0 copy-start.11
  146.3 0.0 copy-start.13
  146.3 0.0 copy-start.14
  146.3 0.0 copy-start.3
  146.3 0.0 copy-start.9
  146.3 0.0 copy-start.10
  146.3 0.0 copy-done
  146.3 0.0 copy-start.2
  146.4 0.0 copy-start.7
  146.4 0.0 copy-start.8
  146.4 0.0 copy-start.15
  146.4 0.0 copy-start.16
  146.4 0.0 copy-start.17
  146.4 2.5 %convert_element_type.8 = f32[8,384,384]{2,1,0:T(8,128)} convert(bf16[8,384,384]{2,1,0:T(8,128)(2,1)S(1)} %copy-done) | non-fusion elementwise | flops 1179648 | bytes 7077888 | tf_op jit(solution)/shard_map/convert_element_type | solution.py:728
  148.9 0.0 copy-done.1
  148.9 0.1 slice_select_fusion.2
  149.1 0.0 copy-done.4
  149.1 0.0 copy-done.5
  149.1 0.0 copy-done.6
  149.1 0.7 multiply_subtract_fusion.2
  149.8 0.0 copy-done.11
  149.8 0.0 copy-done.13
  149.8 0.0 copy-done.14
  149.8 0.6 multiply_subtract_fusion.3
  150.5 0.0 copy-done.3
  150.5 0.0 copy-done.9
  150.5 0.0 copy-done.10
  150.5 0.8 multiply_subtract_fusion.1
  151.3 0.0 copy-done.2
  151.3 0.0 copy-done.7
  151.3 0.0 copy-done.8
  151.3 0.8 multiply_subtract_fusion
  152.1 0.0 copy-done.15
  152.1 0.0 copy-done.16
  152.1 0.0 copy-done.17
  152.1 1.4 multiply_subtract_fusion.4
  (13 shorter events, 0.1 us)
Async XLA Ops:
  8.0 0.6 copy-start.12
  141.9 4.4 %copy-start = (bf16[8,384,384]{2,1,0:T(8,128)(2,1)S(1)}, bf16[8,384,384]{2,1,0:T(8,128)(2,1)}, u32[]{:S(2)}) copy-start(bf16[8,384,384]{2,1,0:T(8,128)(2,1)} %get-tuple-element.27) | copy-start | bytes 7077892
  146.3 2.7 %copy-start.1 = (f32[48,1152]{1,0:T(8,128)S(1)}, f32[48,1152]{1,0:T(8,128)}, u32[]{:S(2)}) copy-start(f32[48,1152]{1,0:T(8,128)} %get-tuple-element.28) | copy-start | bytes 663556
  146.3 2.8 %copy-start.4 = (f32[3,24,192]{2,1,0:T(8,128)S(1)}, f32[3,24,192]{2,1,0:T(8,128)}, u32[]{:S(2)}) copy-start(f32[3,24,192]{2,1,0:T(8,128)} %param.21) | copy-start | bytes 165892
  146.3 2.8 %copy-start.5 = (f32[3,24,192]{2,1,0:T(8,128)S(1)}, f32[3,24,192]{2,1,0:T(8,128)}, u32[]{:S(2)}) copy-start(f32[3,24,192]{2,1,0:T(8,128)} %param.26) | copy-start | bytes 165892
  146.3 2.8 %copy-start.6 = (f32[3,24,192]{2,1,0:T(8,128)S(1)}, f32[3,24,192]{2,1,0:T(8,128)}, u32[]{:S(2)}) copy-start(f32[3,24,192]{2,1,0:T(8,128)} %param.31) | copy-start | bytes 165892
  146.3 3.6 %copy-start.11 = (f32[192,24]{0,1:T(8,128)S(1)}, f32[192,24]{0,1:T(8,128)}, u32[]{:S(2)}) copy-start(f32[192,24]{0,1:T(8,128)} %param.22) | copy-start | bytes 55300
  146.3 3.6 %copy-start.13 = (f32[192,24]{0,1:T(8,128)S(1)}, f32[192,24]{0,1:T(8,128)}, u32[]{:S(2)}) copy-start(f32[192,24]{0,1:T(8,128)} %param.27) | copy-start | bytes 55300
  146.3 3.5 %copy-start.14 = (f32[192,24]{0,1:T(8,128)S(1)}, f32[192,24]{0,1:T(8,128)}, u32[]{:S(2)}) copy-start(f32[192,24]{0,1:T(8,128)} %param.32) | copy-start | bytes 55300
  146.3 4.2 %copy-start.3 = (f32[24,768]{1,0:T(8,128)S(1)}, f32[24,768]{1,0:T(8,128)}, u32[]{:S(2)}) copy-start(f32[24,768]{1,0:T(8,128)} %param.23) | copy-start | bytes 221188
  146.3 4.2 %copy-start.9 = (f32[24,768]{1,0:T(8,128)S(1)}, f32[24,768]{1,0:T(8,128)}, u32[]{:S(2)}) copy-start(f32[24,768]{1,0:T(8,128)} %param.28) | copy-start | bytes 221188
  146.3 4.2 %copy-start.10 = (f32[24,768]{1,0:T(8,128)S(1)}, f32[24,768]{1,0:T(8,128)}, u32[]{:S(2)}) copy-start(f32[24,768]{1,0:T(8,128)} %param.33) | copy-start | bytes 221188
  146.3 5.0 %copy-start.2 = (f32[768,24]{0,1:T(8,128)S(1)}, f32[768,24]{0,1:T(8,128)}, u32[]{:S(2)}) copy-start(f32[768,24]{0,1:T(8,128)} %param.24) | copy-start | bytes 221188
  146.4 5.0 %copy-start.7 = (f32[768,24]{0,1:T(8,128)S(1)}, f32[768,24]{0,1:T(8,128)}, u32[]{:S(2)}) copy-start(f32[768,24]{0,1:T(8,128)} %param.29) | copy-start | bytes 221188
  146.4 5.0 %copy-start.8 = (f32[768,24]{0,1:T(8,128)S(1)}, f32[768,24]{0,1:T(8,128)}, u32[]{:S(2)}) copy-start(f32[768,24]{0,1:T(8,128)} %param.34) | copy-start | bytes 221188
  146.4 5.8 %copy-start.15 = (f32[2,24]{1,0:T(2,128)S(1)}, f32[2,24]{1,0:T(2,128)}, u32[]{:S(2)}) copy-start(f32[2,24]{1,0:T(2,128)} %param.25) | copy-start | bytes 580
  146.4 5.7 %copy-start.16 = (f32[2,24]{1,0:T(2,128)S(1)}, f32[2,24]{1,0:T(2,128)}, u32[]{:S(2)}) copy-start(f32[2,24]{1,0:T(2,128)} %param.30) | copy-start | bytes 580
  146.4 5.7 %copy-start.17 = (f32[2,24]{1,0:T(2,128)S(1)}, f32[2,24]{1,0:T(2,128)}, u32[]{:S(2)}) copy-start(f32[2,24]{1,0:T(2,128)} %param.35) | copy-start | bytes 580

commit v2 on v1

v2 whole, which is shorter than its diff:
```python
import functools
import types

import jax
import jax.numpy as jnp
from jax import lax
from jax.experimental import pallas as pl
from jax.experimental.pallas import tpu as pltpu
from jax.sharding import PartitionSpec as P

MESH = pl.DeviceIdType.MESH
bf = jnp.bfloat16
f32 = jnp.float32
S = 384
D = 384
NN=(((1,),(0,)),((),())); NT=(((1,),(1,)),((),())); TN=(((0,),(0,)),((),()))
def dot(a,b,dn=NN): return lax.dot_general(a,b,dn,preferred_element_type=f32)

def ln_stats(x):
    c = x - jnp.mean(x,axis=-1,keepdims=True)
    r = lax.rsqrt(jnp.mean(c*c,axis=-1,keepdims=True)+1e-6)
    return c*r, r

def gelu_parts(u):
    z = jnp.abs(u)*0.7071067811865476
    t = 1.0/(1.0+0.3275911*z)
    poly = t*(0.127414796 + t*(-0.142248368 + t*(0.7107068705 + t*(-0.7265760135 + t*0.5307027145))))
    E = jnp.exp(u*u*-0.5)
    h = poly*E
    phi = jnp.where(u>=0, 1.0-h, h)
    return phi, E*0.3989422804014327

def stack2(t, lo):
    z=jnp.zeros_like(t)
    return jnp.concatenate([jnp.where(lo,t,z),jnp.where(lo,z,t)],axis=0)

def unstackT(t):
    return jnp.concatenate([t[:64,:S],t[64:,S:]],axis=0).T

def a1(img, R, count):
    xh,_ = ln_stats(R.x[img])
    h1=(xh*R.g1).astype(bf)
    R.h1[img]=h1
    for b in range(3):
        for m in range(3):
            c=m*384+128*b
            R.qkv[img,:,c:c+128]=dot(h1,R.wqkv[:,c:c+128]).astype(bf)
    lo=lax.broadcasted_iota(jnp.int32,(S,128),1)<64
    for b in range(3):
        q=R.qkv[img,:,128*b:128*b+128]*jnp.asarray(0.125,bf)
        k=R.qkv[img,:,384+128*b:512+128*b]
        v=R.qkv[img,:,768+128*b:896+128*b]
        q2=stack2(q,lo)
        s=dot(k,q2,NT)
        key=lax.broadcasted_iota(jnp.int32,(128,2*S),0)
        s=jnp.concatenate([s[:256],jnp.where(key<count,s[256:],-1e30)],axis=0)
        mx=jnp.max(s,axis=0,keepdims=True)
        e=jnp.exp(s-mx)
        p=e*(1.0/jnp.sum(e,axis=0,keepdims=True))
        R.p[img,b]=p
        oT=dot(v,p.astype(bf),TN)
        R.o[img,:,128*b:128*b+128]=unstackT(oT).astype(bf)

CH=512
def a2(img, R):
    o=R.o[img]; x=R.x[img]; g=R.g[img]
    y1=x+dot(o,R.wo[...],NT)
    xh2,r2=ln_stats(y1)
    h2=(xh2*R.g2).astype(bf)
    dl=g.astype(bf)
    bo=y1; dh2=jnp.zeros((S,D),f32)
    for c0 in range(0,1536,CH):
        c=slice(c0,c0+CH)
        u=dot(h2,R.wu[:,c])
        da=dot(dl,R.wd[:,c])
        phi,ph=gelu_parts(u)
        a=(u*phi).astype(bf)
        du=(da*(phi+u*ph)).astype(bf)
        bo=bo+dot(a,R.wd[:,c],NT)
        dh2=dh2+dot(du,R.wu[:,c],NT)
        R.Gu[:,c]=R.Gu[:,c]+dot(h2,du,TN)
        R.Gd[:,c]=R.Gd[:,c]+dot(dl,a,TN)
    R.bo[img]=bo.astype(R.bo.dtype)
    e=dh2*R.g2
    m1=jnp.mean(e,axis=-1,keepdims=True)
    m2=jnp.mean(e*xh2,axis=-1,keepdims=True)
    dy=g+r2*(e-m1-xh2*m2)
    R.dy[img]=dy
    R.gn[1:2,:]=R.gn[1:2,:]+jnp.sum(dh2*xh2,axis=0,keepdims=True)
    R.Go[...]=R.Go[...]+dot(dy.astype(bf),o,TN)

def cc(img, R):
    dy=R.dy[img]
    dm=dy.astype(bf)
    h1=R.h1[img]
    lo=lax.broadcasted_iota(jnp.int32,(S,128),1)<64
    dh1=jnp.zeros((S,D),f32)
    for b in range(3):
        sl=slice(128*b,128*b+128)
        do=dot(dm,R.wo[:,sl]).astype(bf)
        do2=stack2(do,lo)
        q2=stack2(R.qkv[img,:,sl]*jnp.asarray(0.125,bf),lo)
        k=R.qkv[img,:,384+128*b:512+128*b]
        v=R.qkv[img,:,768+128*b:896+128*b]
        p=R.p[img,b]
        dv=dot(p.astype(bf),do2).astype(bf)
        dp=dot(v,do2,NT)
        inner=jnp.sum(p*dp,axis=0,keepdims=True)
        ds=(p*(dp-inner)).astype(bf)
        dk=dot(ds,q2).astype(bf)
        dq=(unstackT(dot(k,ds,TN))*0.125).astype(bf)
        R.dqkv[:,sl]=dq; R.dqkv[:,384+128*b:512+128*b]=dk; R.dqkv[:,768+128*b:896+128*b]=dv
    dqkv=R.dqkv[...]
    R.Gqkv[...]=R.Gqkv[...]+dot(h1,dqkv,TN)
    dh1=dot(dqkv,R.wqkv[...],NT)
    xh1,r1=ln_stats(R.x[img])
    e=dh1*R.g1
    m1=jnp.mean(e,axis=-1,keepdims=True)
    m2=jnp.mean(e*xh1,axis=-1,keepdims=True)
    ig=dy+r1*(e-m1-xh1*m2)
    R.ig[img]=ig.astype(R.ig.dtype)
    R.gn[0:1,:]=R.gn[0:1,:]+jnp.sum(dh1*xh1,axis=0,keepdims=True)


STEP = 5
EPS_ADAM = 1e-08
BETA_FIRST = 0.5
BETA_SECOND = 0.5
DECAY_MATRIX = 0.01
RATE_QKV = 0.05
RATE_OUT = 0.2
RATE_UP = 0.05
RATE_DOWN = 0.03
RATE_NORM = 0.3


class Plan:
    def __init__(self, dp, mp, rows, images):
        assert mp == 2 and dp >= 4 and dp & (dp - 1) == 0
        self.dp, self.mp, self.rows = dp, mp, rows
        self.bits = dp.bit_length() - 1
        self.slots = dp * mp
        self.folded = -(-2 * rows // 16) * 16
        self.images = images
        self.here = images // mp
        high = [("dp", b) for b in range(2, self.bits)]
        high = [high] if high else []
        x, y, core = [("mp", 0)], [("dp", 1)], [("dp", 0)]
        self.gather = [
            (0, 2, high + [x, y, core]),
            (2, 1, high + [y, x, core]),
            (3, 4, high + [y, x, core]),
            (7, 2, high + [x, y, core]),
        ]
        self.scatter = [
            (0, 2, [x] + high + [y, core]),
            (2, 1, [x, y] + high + [core]),
            (3, 4, [x] + high + [y, core]),
            (7, 2, [x, y] + high + [core]),
        ]
        self.gains = high + [y, core]
        self.sums = [core, y] + high + [x]

    def copies(self, stages):
        return sum(2 ** len(e) - 1 for e in stages)

    def partners(self):
        found = []
        for stages in [e[2] for e in self.gather + self.scatter] + [self.gains, self.sums]:
            for stage in stages:
                for d in range(1, 2 ** len(stage)):
                    flip = sorted(e for m, e in enumerate(stage) if (d >> m) & 1)
                    if flip not in found:
                        found.append(flip)
        return found


def slot_of(stages, i, j):
    total = 0
    for t, (axis, b) in enumerate(e for stage in stages for e in stage):
        bit = j if axis == "mp" else (i // 2**b) % 2
        total = total + bit * 2**t
    return total


class Place:
    def __init__(self):
        self.i = lax.axis_index("dp")
        self.j = lax.axis_index("mp")

    def bit(self, axis_bit):
        axis, b = axis_bit
        return self.j if axis == "mp" else lax.rem(self.i // 2**b, 2)

    def partner(self, flip):
        where = {}
        for axis, b in flip:
            if axis == "mp":
                where["mp"] = 1 - self.j
            else:
                step = 2**b - 2 ** (b + 1) * self.bit((axis, b))
                where["dp"] = where.get("dp", self.i) + step
        return where

    def number(self, bits, d=0):
        total = 0
        for m, e in enumerate(bits):
            bit = 1 - self.bit(e) if (d >> m) & 1 else self.bit(e)
            total = total + bit * 2**m
        return total


def remote(src, dst, send, recv, where):
    return pltpu.make_async_remote_copy(
        src_ref=src, dst_ref=dst, send_sem=send, recv_sem=recv, device_id=where, device_id_type=MESH
    )


class Exchange:
    def __init__(self, place, stages, send, recv):
        self.place, self.stages, self.send, self.recv = place, stages, send, recv
        self.before, self.first = [], []
        bits = copies = 0
        for stage in stages:
            self.before.append(bits)
            self.first.append(copies)
            bits += len(stage)
            copies += 2 ** len(stage) - 1

    def others(self, s):
        return range(1, 2 ** len(self.stages[s]))

    def flip(self, s, d):
        return [e for m, e in enumerate(self.stages[s]) if (d >> m) & 1]

    def link(self, s, d, src, dst):
        n = self.first[s] + d - 1
        return remote(
            src, dst, self.send.at[n], self.recv.at[n], self.place.partner(self.flip(s, d))
        )

    def start(self, s):
        for d in self.others(s):
            self.copy(s, d).start()

    def wait(self, s):
        for d in self.others(s):
            self.copy(s, d).wait_recv()

    def finish(self):
        for s in range(len(self.stages)):
            for d in self.others(s):
                self.copy(s, d).wait_send()


class Gather(Exchange):
    def __init__(self, place, stages, buf, send, recv):
        super().__init__(place, stages, send, recv)
        self.buf = buf
        self.slot = place.number([e for stage in stages for e in stage])

    def copy(self, s, d):
        size = 2 ** self.before[s]
        part = self.buf.at[pl.ds(self.slot - lax.rem(self.slot, size), size)]
        return self.link(s, d, part, part)


class Scatter(Exchange):
    def __init__(self, place, stages, total, out, came, send, recv):
        super().__init__(place, stages, send, recv)
        self.total, self.out, self.came = total, out, came
        self.top = len(stages) - 1
        self.own = place.number([e for stage in stages[:-1] for e in stage])

    def copy(self, s, d):
        size = 2 ** self.before[s]
        part = pl.ds(size * d, size)
        return self.link(s, d, self.out.at[part], self.came.at[part])

    def held(self, s, d=0):
        size = 2 ** self.before[s]
        base = self.own - lax.rem(self.own, size * 2 ** len(self.stages[s]))
        return pl.ds(base + size * self.place.number(self.stages[s], d), size)

    def start(self, s):
        if s < self.top:
            size = 2 ** self.before[s]
            for d in self.others(s):
                self.out[pl.ds(size * d, size)] = self.total[self.held(s, d)].astype(bf)
        super().start(s)

    def add(self, s):
        size = 2 ** self.before[s]
        self.wait(s)
        keep = pl.ds(0, size) if s == self.top else self.held(s)
        value = self.total[keep]
        for d in self.others(s):
            value = value + self.came[pl.ds(size * d, size)].astype(f32)
        self.total[keep] = value


class Sum(Exchange):
    def __init__(self, place, stages, bufs, send, recv):
        super().__init__(place, stages, send, recv)
        self.bufs = bufs

    def copy(self, s, d):
        part = self.bufs.at[s, self.place.number(self.stages[s])]
        return self.link(s, d, part, part)

    def begin(self, s, value):
        self.bufs[s, self.place.number(self.stages[s])] = value
        self.start(s)

    def total(self, s):
        self.wait(s)
        value = self.bufs[s, 0]
        for d in self.others(s):
            value = value + self.bufs[s, d]
        return value


def low_half(rows):
    return lax.broadcasted_iota(jnp.int32, (rows, 128), 1) < 64


def unpack(plan, groups, bufs, R, which):
    rows = plan.rows
    step = 16
    while step % rows and (step // 16) < 64:
        step += 16
    per = max(step // rows, 1)
    if (per * rows) % 16:
        raise ValueError("rows")
    first, last = (0, 3) if which == "A" else (3, 9)
    for m in range(plan.dp // per):
        tops, bottoms = [[], []], [[], []]
        for j in range(2):
            for f in range(first, last):
                g = next(n for n, e in enumerate(groups) if e[0] <= f < e[0] + e[1])
                lane = 128 * (f - groups[g][0])
                parts = [
                    bufs[g][slot_of(groups[g][2], m * per + n, j), :, lane : lane + 128].astype(f32)
                    for n in range(per)
                ]
                tops[j].append(jnp.concatenate([q[:rows] for q in parts], axis=0))
                bottoms[j].append(jnp.concatenate([q[rows : 2 * rows] for q in parts], axis=0))
        c0, c1 = tops[0] + bottoms[0], tops[1] + bottoms[1]
        size = per * rows
        lo = low_half(size)
        at = slice(m * size, (m + 1) * size)

        def put(ref, block, value):
            ref[at, 128 * block : 128 * block + 128] = value.astype(bf)

        if which == "A":
            for n in range(3):
                put(R.wqkv, 3 * n, c0[n])
                put(R.wqkv, 3 * n + 1, jnp.where(lo, c0[3 + n], c1[3 + n]))
                put(R.wqkv, 3 * n + 2, c1[n])
            put(R.wu, 10, jnp.where(lo, c1[3], c0[3]))
            put(R.wu, 11, jnp.where(lo, c1[4], c0[4]))
            put(R.wd, 10, jnp.where(lo, c1[5], c0[5]))
        else:
            put(R.wo, 0, c0[0])
            put(R.wo, 1, jnp.where(lo, c0[1], c1[1]))
            put(R.wo, 2, c1[0])
            put(R.wd, 11, jnp.where(lo, c1[1], c0[1]))
            for n in range(5):
                put(R.wu, n, c0[2 + n])
                put(R.wu, 5 + n, c1[2 + n])
                put(R.wd, n, c0[7 + n])
                put(R.wd, 5 + n, c1[7 + n])


def pack(plan, groups, scatters, R, core, which):
    rows = plan.rows
    lo = low_half(2 * rows)
    first, last = (0, 3) if which == "A" else (3, 9)
    for r in range(plan.dp // 2):
        at = slice(2 * r * rows, 2 * (r + 1) * rows)

        def get(ref, block):
            return ref[at, 128 * block : 128 * block + 128]

        def piece(j, n):
            if which == "A":
                if n < 3:
                    return get(R.Gqkv, 3 * n + 2 * j)
                own = get(R.Gqkv, 3 * (n - 3) + 1)
                fill = get(R.Gu, 7 + n) if n < 5 else get(R.Gd, 10)
            elif n == 0:
                return get(R.Go, 2 * j)
            elif n == 1:
                own, fill = get(R.Go, 1), get(R.Gd, 11)
            elif n < 7:
                return get(R.Gu, n - 2 + 5 * j)
            else:
                return get(R.Gd, n - 7 + 5 * j)
            return jnp.where(lo, own, fill) if j == 0 else jnp.where(lo, fill, own)

        for j in range(2):
            for f in range(first, last):
                g = next(n for n, e in enumerate(groups) if e[0] <= f < e[0] + e[1])
                lane = 128 * (f - groups[g][0])
                n = f - first
                top, bottom = piece(j, n), piece(j, n + last - first)
                even = jnp.concatenate([top[:rows], bottom[:rows]], axis=0)
                odd = jnp.concatenate([top[rows:], bottom[rows:]], axis=0)
                if plan.folded > 2 * rows:
                    none = jnp.zeros((plan.folded - 2 * rows, 128), f32)
                    even = jnp.concatenate([even, none], axis=0)
                    odd = jnp.concatenate([odd, none], axis=0)
                slot = slot_of(groups[g][2][:-1], 2 * r, j)
                half = plan.slots // 2
                scatters[g].out[half + slot, :, lane : lane + 128] = jnp.where(
                    core == 0, odd, even
                ).astype(bf)
                scatters[g].total[slot, :, lane : lane + 128] = jnp.where(core == 0, even, odd)


def own_chunk(plan, j, qkv, out_w, up, down):
    oT, dT = out_w, down

    def mix(own, fill):
        return jnp.where(
            j == 0,
            jnp.concatenate([own, fill], axis=1),
            jnp.concatenate([fill, own], axis=1),
        )

    part_a = [qkv[n, :, :128] for n in range(3)] + [
        mix(qkv[0, :, 128:192], up[:, 640:704]),
        mix(qkv[1, :, 128:192], up[:, 704:768]),
        mix(qkv[2, :, 128:192], dT[:, 640:704]),
    ]
    part_b = [oT[:, :128], mix(oT[:, 128:192], dT[:, 704:768])]
    part_b += [up[:, 128 * n : 128 * n + 128] for n in range(5)]
    part_b += [dT[:, 128 * n : 128 * n + 128] for n in range(5)]
    pad = plan.folded - 2 * plan.rows
    blocks = []
    for part in (part_a, part_b):
        half = len(part) // 2
        for n in range(half):
            rows = [part[n], part[n + half]]
            if pad:
                rows.append(jnp.zeros((pad, 128), f32))
            blocks.append(jnp.concatenate(rows, axis=0).astype(bf))
    return blocks


def wide_rows(plan, norm):
    values = norm[...].astype(bf).astype(f32)
    values = jnp.concatenate([values, jnp.zeros((2, 128 - plan.rows), f32)], axis=1)
    values = jnp.concatenate([values, jnp.zeros((6, 128), f32)], axis=0)
    return jnp.concatenate([values, jnp.zeros((8, D - 128), f32)], axis=1)


def layer_kernel(plan, *refs):
    it = iter(refs)
    take = lambda n: [next(it) for _ in range(n)]
    counts, inputs, out_grad = take(3)
    weights_in = take(5)
    bo_out, ig_out, grads_out, gn_out = take(4)
    weights = take(5)
    x, g, h1, qkv, p, o, dy, dqkv = take(8)
    wqkv, wo, wu, wd, Gqkv, Go, Gu, Gd, gn = take(9)
    bo, ig = take(2)
    ng, ns = len(plan.gather), len(plan.scatter)
    gbufs = take(ng)
    g_send, g_recv = take(2)
    totals, cames = take(ns), take(ns)
    outs = gbufs
    s_send, s_recv = take(2)
    gains_buf, gains_send, gains_recv = take(3)
    sums_buf, sums_send, sums_recv = take(3)
    load_sem, weight_sem, store_sem, x_send, x_recv = take(5)

    place = Place()
    i, j = place.i, place.j
    here = plan.here

    partners = plan.partners()
    barrier = pltpu.get_barrier_semaphore()
    for flip in partners:
        pl.semaphore_signal(barrier, inc=1, device_id=place.partner(flip), device_id_type=MESH)

    weight_loads = [
        pltpu.make_async_copy(src, dst, weight_sem.at[n])
        for n, (src, dst) in enumerate(zip(weights_in, weights))
    ]
    loads = []
    for n in range(here):
        for k, (src, dst) in enumerate(((inputs, x), (out_grad, g))):
            loads.append(
                pltpu.make_async_copy(src.at[j * here + n], dst.at[n], load_sem.at[k, n])
            )
    for c in weight_loads + loads:
        c.start()

    gathers = [
        Gather(place, stages, gbufs[n], g_send.at[n], g_recv.at[n])
        for n, (_, _, stages) in enumerate(plan.gather)
    ]
    scatters = [
        Scatter(place, stages, totals[n], outs[n], cames[n], s_send.at[n], s_recv.at[n])
        for n, (_, _, stages) in enumerate(plan.scatter)
    ]
    gains = Sum(place, plan.gains, gains_buf, gains_send, gains_recv)
    sums = Sum(place, plan.sums, sums_buf, sums_send, sums_recv)
    first = [c for c, e in zip(gathers, plan.gather) if e[0] < 3]
    second = [c for c, e in zip(gathers, plan.gather) if e[0] >= 3]
    late = [c for c, e in zip(scatters, plan.scatter) if e[0] < 3]
    early = [c for c, e in zip(scatters, plan.scatter) if e[0] >= 3]

    for c in weight_loads:
        c.wait()
    blocks = own_chunk(plan, j, *weights[:4])
    for c, (f, size, _) in zip(gathers, plan.gather):
        for n in range(size):
            c.buf[c.slot, :, 128 * n : 128 * n + 128] = blocks[f + n]
    mine = pltpu.roll(wide_rows(plan, weights[4]), i * plan.rows, 1)

    pl.semaphore_wait(barrier, len(partners))

    stages = len(plan.gather[0][2])
    for s in range(stages):
        for c in first:
            if s:
                c.wait(s - 1)
            c.start(s)
        if s < len(plan.gains):
            gains.begin(s, gains.total(s - 1) if s else mine)
        if 0 < s < stages - 1:
            for c in second:
                if s > 1:
                    c.wait(s - 2)
                c.start(s - 1)
        if s == 0:
            for ref in (Gqkv, Go, Gu, Gd, gn):
                ref[...] = jnp.zeros_like(ref)
    rounded = gains.total(len(plan.gains) - 1)
    R = types.SimpleNamespace(
        x=x, g=g, h1=h1, qkv=qkv, p=p, o=o, dy=dy, dqkv=dqkv, wqkv=wqkv, wo=wo, wu=wu, wd=wd,
        Gqkv=Gqkv, Go=Go, Gu=Gu, Gd=Gd, gn=gn, bo=bo, ig=ig,
    )
    R.g1 = rounded[0:1, :]
    R.g2 = rounded[1:2, :]
    for c in loads:
        c.wait()
    for c in first:
        c.wait(stages - 1)
    for c in second:
        c.wait(stages - 3)
        c.start(stages - 2)
    unpack(plan, plan.gather, gbufs, R, "A")

    def attend(n, carry):
        a1(n, R, counts[j * here + n])

        @pl.when(n == (here - 1) // 2)
        def _():
            for c in second:
                c.wait(stages - 2)
                c.start(stages - 1)

        return carry

    lax.fori_loop(0, here, attend, 0)
    for c in second:
        c.wait(stages - 1)
    unpack(plan, plan.gather, gbufs, R, "B")
    for c in gathers + [gains]:
        c.finish()

    def swap(n, k):
        ref, out = ((bo, bo_out), (ig, ig_out))[k]
        return (
            pltpu.make_async_copy(ref.at[n], out.at[j * here + n], store_sem.at[k, n]),
            remote(
                ref.at[n], out.at[j * here + n], x_send.at[k, n], x_recv.at[k, n], {"mp": 1 - j}
            ),
        )

    def feed(n, carry):
        a2(n, R)
        for c in swap(n, 0):
            c.start()
        return carry

    lax.fori_loop(0, here, feed, 0)

    core = place.bit(("dp", 0))
    pack(plan, plan.scatter, scatters, R, core, "B")
    top = len(plan.scatter[0][2]) - 1
    for c in early:
        c.start(top)

    def advance(group, s):
        for c in group:
            c.add(s)
            if s:
                c.start(s - 1)

    due = {0: top, here - 1: top - 1}

    def back(n, carry):
        cc(n, R)
        for c in swap(n, 1):
            c.start()
        for image, s in due.items():

            @pl.when(n == image)
            def _(s=s):
                advance(early, s)

        return carry

    lax.fori_loop(0, here, back, 0)

    pack(plan, plan.scatter, scatters, R, core, "A")
    for c in late:
        c.start(top)
    sums.begin(0, gn[...])
    s_early = top - 2
    for s in range(top, -1, -1):
        advance(late, s)
        step = top - s
        value = sums.total(step)
        if step + 1 < len(plan.sums):
            sums.begin(step + 1, value)
        if s_early >= 0:
            advance(early, s_early)
            s_early -= 1
    for c, (f, size, _) in zip(scatters, plan.scatter):
        grads_out[:, 128 * f : 128 * (f + size)] = c.total[c.own]
    gn_out[...] = value

    for c in scatters + [sums]:
        c.finish()
    for n in range(here):
        for k in range(2):
            own, away = swap(n, k)
            own.wait()
            away.wait()


def run_layer(plan, counts, inputs, out_grad, weights):
    here, slots, folded = plan.here, plan.slots, plan.folded
    vmem = pl.BlockSpec(memory_space=pltpu.VMEM)
    hbm = pl.BlockSpec(memory_space=pl.ANY)
    dma = pltpu.SemaphoreType.DMA
    out = jax.ShapeDtypeStruct
    ng, ns = len(plan.gather), len(plan.scatter)
    lanes_g = [128 * e[1] for e in plan.gather]
    assert [e[:2] for e in plan.gather] == [e[:2] for e in plan.scatter]
    lanes_s = [128 * e[1] for e in plan.scatter]
    copies_g = max(plan.copies(e[2]) for e in plan.gather)
    copies_s = max(plan.copies(e[2]) for e in plan.scatter)

    def sum_scratch(stages):
        return [
            pltpu.VMEM((len(stages), max(2 ** len(e) for e in stages), 8, D), f32),
            dma((plan.copies(stages),)),
            dma((plan.copies(stages),)),
        ]

    scratch = [pltpu.VMEM(w.shape, f32) for w in weights]
    scratch += [
        pltpu.VMEM((here, S, D), f32),
        pltpu.VMEM((here, S, D), f32),
        pltpu.VMEM((here, S, D), bf),
        pltpu.VMEM((here, S, 3 * D), bf),
        pltpu.VMEM((here, 3, S, 2 * S), f32),
        pltpu.VMEM((here, S, D), bf),
        pltpu.VMEM((here, S, D), f32),
        pltpu.VMEM((S, 3 * D), bf),
        pltpu.VMEM((D, 3 * D), bf),
        pltpu.VMEM((D, D), bf),
        pltpu.VMEM((D, 4 * D), bf),
        pltpu.VMEM((D, 4 * D), bf),
        pltpu.VMEM((D, 3 * D), f32),
        pltpu.VMEM((D, D), f32),
        pltpu.VMEM((D, 4 * D), f32),
        pltpu.VMEM((D, 4 * D), f32),
        pltpu.VMEM((8, D), f32),
        pltpu.VMEM((here, S, D), bf),
        pltpu.VMEM((here, S, D), bf),
    ]
    scratch += [pltpu.VMEM((slots, folded, n), bf) for n in lanes_g]
    scratch += [dma((ng, copies_g)), dma((ng, copies_g))]
    scratch += [pltpu.VMEM((slots // 2, folded, n), f32) for n in lanes_s]
    scratch += [pltpu.VMEM((slots, folded, n), bf) for n in lanes_s]
    scratch += [dma((ns, copies_s)), dma((ns, copies_s))]
    scratch += sum_scratch(plan.gains) + sum_scratch(plan.sums)
    scratch += [
        dma((2, here)),
        dma((len(weights),)),
        dma((2, here)),
        dma((2, here)),
        dma((2, here)),
    ]
    return pl.pallas_call(
        functools.partial(layer_kernel, plan),
        out_shape=[
            out(inputs.shape, bf),
            out(inputs.shape, bf),
            out((folded, 9 * 128), f32),
            out((8, D), f32),
        ],
        in_specs=[pl.BlockSpec(memory_space=pltpu.SMEM)] + [hbm] * (2 + len(weights)),
        out_specs=[hbm, hbm, vmem, vmem],
        scratch_shapes=scratch,
        compiler_params=pltpu.CompilerParams(
            collective_id=0, has_side_effects=True, vmem_limit_bytes=63 << 20
        ),
        name="layer",
    )(counts, inputs, out_grad, *weights)


def adamw_update(weight, gradient, first_moment, second_moment, step_rate, decay_rate):
    first_next = BETA_FIRST * first_moment + (1.0 - BETA_FIRST) * gradient
    second_next = BETA_SECOND * second_moment + (1.0 - BETA_SECOND) * gradient * gradient
    first_fixed = first_next / (1.0 - BETA_FIRST**STEP)
    second_fixed = second_next / (1.0 - BETA_SECOND**STEP)
    weight_next = weight - step_rate * (
        first_fixed / (jnp.sqrt(second_fixed) + EPS_ADAM) + decay_rate * weight
    )
    return (weight_next, first_next, second_next)


def own_gradients(plan, i, j, grads, sums):
    rows = plan.rows

    def block(f, lower):
        return grads[rows * lower : rows * (lower + 1), 128 * f : 128 * f + 128]

    part_a = [block(n, 0) for n in range(3)] + [block(n, 1) for n in range(3)]
    part_b = [block(3 + n, 0) for n in range(6)] + [block(3 + n, 1) for n in range(6)]

    def split(value):
        left, right = value[:, :64], value[:, 64:]
        return jnp.where(j == 0, left, right), jnp.where(j == 0, right, left)

    own, fill = zip(*[split(e) for e in part_a[3:] + part_b[1:2]])
    qkv = [jnp.concatenate([part_a[n], own[n]], axis=1) for n in range(3)]
    out_w = jnp.concatenate([part_b[0], own[3]], axis=1)
    up = jnp.concatenate(part_b[2:7] + [fill[0], fill[1]], axis=1)
    down = jnp.concatenate(part_b[7:12] + [fill[2], fill[3]], axis=1)
    norm = pltpu.roll(sums, D - i * rows, 1)[:2, :rows]
    return qkv, out_w, up, down, norm


RATES = (
    (RATE_QKV, DECAY_MATRIX),
    (RATE_OUT, DECAY_MATRIX),
    (RATE_UP, DECAY_MATRIX),
    (RATE_DOWN, DECAY_MATRIX),
    (RATE_NORM, 0.0),
)


def finish_kernel(plan, *refs):
    it = iter(refs)
    take = lambda n: [next(it) for _ in range(n)]
    bo_in, ig_in = take(2)
    small_in = take(17)
    bo_out, ig_out = take(2)
    small_out = take(20)
    low, full = take(2)
    small = take(17)
    results = take(20)
    in_sem, small_sem, out_sem, result_sem = take(4)
    i, j = lax.axis_index("dp"), lax.axis_index("mp")
    n_images = plan.images

    small_loads = [
        pltpu.make_async_copy(src, dst, small_sem.at[n])
        for n, (src, dst) in enumerate(zip(small_in, small))
    ]
    loads, stores = [], []
    for n in range(n_images):
        for k, (src, dst) in enumerate(((bo_in, bo_out), (ig_in, ig_out))):
            loads.append(pltpu.make_async_copy(src.at[n], low.at[k, n], in_sem.at[k, n]))
            stores.append(pltpu.make_async_copy(full.at[k, n], dst.at[n], out_sem.at[k, n]))
    half = len(loads) // 2
    for c in loads[:half] + small_loads + loads[half:]:
        c.start()

    def convert(n):
        k, image = n % 2, n // 2
        loads[n].wait()
        full[k, image] = low[k, image].astype(f32)
        stores[n].start()

    for n in range(half):
        convert(n)
    for c in small_loads:
        c.wait()
    gradients = own_gradients(plan, i, j, small[0][...], small[1][...])
    for n in range(5):
        weight, first, second = small[2 + n], small[7 + n], small[12 + n]
        for c in range(3) if n == 0 else [...]:
            gradient = gradients[0][c] if n == 0 else gradients[n]
            new = adamw_update(weight[c], gradient, first[c], second[c], *RATES[n])
            for k in range(3):
                results[5 * k + n][c] = new[k]
            results[15 + n][c] = gradient
    result_stores = [
        pltpu.make_async_copy(src, dst, result_sem.at[n])
        for n, (src, dst) in enumerate(zip(results, small_out))
    ]
    for c in result_stores:
        c.start()
    for n in range(half, len(loads)):
        convert(n)
    for c in stores + result_stores:
        c.wait()


def run_finish(plan, bo, ig, small):
    hbm = pl.BlockSpec(memory_space=pl.ANY)
    dma = pltpu.SemaphoreType.DMA
    out = jax.ShapeDtypeStruct
    weights = [e.shape for e in small[2:7]]
    return pl.pallas_call(
        functools.partial(finish_kernel, plan),
        out_shape=[out(bo.shape, f32), out(ig.shape, f32)] + [out(e, f32) for e in weights * 4],
        in_specs=[hbm] * 19,
        out_specs=[hbm] * 22,
        scratch_shapes=[pltpu.VMEM((2,) + bo.shape, bf), pltpu.VMEM((2,) + bo.shape, f32)]
        + [pltpu.VMEM(e.shape, f32) for e in small]
        + [pltpu.VMEM(e, f32) for e in weights * 4]
        + [dma((2, plan.images)), dma((17,)), dma((2, plan.images)), dma((20,))],
        compiler_params=pltpu.CompilerParams(vmem_limit_bytes=62 << 20),
        name="finish",
    )(bo, ig, *small)


def shards(dp, mp, inputs, out_grad, counts, *state):
    plan = Plan(dp, mp, state[2].shape[0], inputs.shape[0])
    turn = lambda arrays: tuple(e.T if n % 5 in (1, 3) else e for n, e in enumerate(arrays))
    state = turn(state)
    bo, ig, grads, sums = run_layer(plan, counts, inputs, out_grad, state[:5])
    bo, ig, *new = run_finish(plan, bo, ig, (grads, sums) + state)
    return (bo, ig) + turn(new)


def solution(mesh):
    stored = (
        P(None, "dp", "mp"),
        P("mp", "dp"),
        P("dp", "mp"),
        P("mp", "dp"),
        P(None, "dp"),
    )
    images = P("dp", None, None)
    return jax.shard_map(
        functools.partial(shards, mesh.shape["dp"], mesh.shape["mp"]),
        mesh=mesh,
        in_specs=(images, images, P("dp")) + stored * 3,
        out_specs=(images, images) + stored * 4,
        check_vma=False,
    )
```

time: 154 us -> 115 us (0.75)
  Pallas kernels: 133 us -> 114 us
  other arithmetic: 12.7 us -> 0 us
  local copies, waits for them, and re-layouts: 6.55 us -> 0 us
    pallas_call x1, Pallas kernels: 133 us -> 107 us  [run_layer(): pl.pallas_call(functools.partial(layer_kernel, plan), out_shape=[out(inpu...]
    pallas_call x0 -> x1, Pallas kernels: none -> 7.51 us  [run_finish(): pl.pallas_call(functools.partial(finish_kernel, plan), out_shape=[out(bo....]
    convert_element_type x2 -> x0, other arithmetic: 6.83 us -> none  [the longest x1 4.32 us: shards(): bo.astype(f32)]
    slice x15 -> x0, local copies, waits for them, and re-layouts: 4.84 us -> none  [the longest x1 0.86 us: shards(): dT[:, 640:704]]
    sub x5 -> x0, other arithmetic: 4.31 us -> none  [adamw_update(): weight - step_rate * (first_fixed / (jnp.sqrt(second_fixed) + EPS_ADAM) +...]
where the time goes in v2:
time: 115 us
  Pallas kernels  114 us (99%)
    pallas_call x1, Pallas kernels, run_layer(): pl.pallas_call(functools.partial(layer_kernel, plan), out_shape=[out(inpu...  107 us
    pallas_call x1, Pallas kernels, run_finish(): pl.pallas_call(functools.partial(finish_kernel, plan), out_shape=[out(bo....  7.51 us

profile of v2, /device:TPU:0, one launch (start us, length us, event | category | flops | bytes accessed | tf_op | source)
XLA Modules:
  0.0 115.1 jit_solution(9700071558143588866)
XLA Ops:
  0.7 106.8 %layer.1 = (bf16[8,384,384]{2,1,0:T(8,128)(2,1)}, bf16[8,384,384]{2,1,0:T(8,128)(2,1)}, f32[48,1152]{1,0:T(8,128)}, f32[8,384]{1,0:T(8,128)}) custom-call(s32[8]{0:T(128)} %refs_0_.1, f32[8,384,384]{2,1,0:T(8,128)} %refs_1_.1, f32[8,384,384]{2,1,0:T(8,128)} %refs_2_.1, f32[3,24,192]{2,1,0:T(8,128)} %refs_4_.1, f32[24,192]{1,0:T(8,128)} %bitcast.16, ...), custom_call_target="tpu_custom_call" | custom-call | tf_op jit(solution)/shard_map/layer/pallas_call | solution.py:703
  107.4 7.5 %finish.1 = (f32[8,384,384]{2,1,0:T(8,128)}, f32[8,384,384]{2,1,0:T(8,128)}, f32[3,24,192]{2,1,0:T(8,128)}, f32[24,192]{1,0:T(8,128)}, f32[24,768]{1,0:T(8,128)}...) custom-call(bf16[8,384,384]{2,1,0:T(8,128)(2,1)} %get-tuple-element., ...), custom_call_target="tpu_custom_call" | custom-call | tf_op jit(solution)/shard_map/finish/pallas_call | solution.py:826

commit v3 on v2

--- a/solution.py
+++ b/solution.py
@@ -38,8 +38,7 @@
     return jnp.concatenate([t[:64,:S],t[64:,S:]],axis=0).T
 
 def a1(img, R, count):
-    xh,_ = ln_stats(R.x[img])
-    h1=(xh*R.g1).astype(bf)
+    h1=(R.xh[img]*R.g1).astype(bf)
     R.h1[img]=h1
     for b in range(3):
         for m in range(3):
@@ -57,12 +56,13 @@
         mx=jnp.max(s,axis=0,keepdims=True)
         e=jnp.exp(s-mx)
         p=e*(1.0/jnp.sum(e,axis=0,keepdims=True))
+        p=p.astype(bf)
         R.p[img,b]=p
-        oT=dot(v,p.astype(bf),TN)
+        oT=dot(v,p,TN)
         R.o[img,:,128*b:128*b+128]=unstackT(oT).astype(bf)
 
 CH=512
-def a2(img, R):
+def a2(img, R, between=lambda k: None):
     o=R.o[img]; x=R.x[img]; g=R.g[img]
     y1=x+dot(o,R.wo[...],NT)
     xh2,r2=ln_stats(y1)
@@ -80,6 +80,7 @@
         dh2=dh2+dot(du,R.wu[:,c],NT)
         R.Gu[:,c]=R.Gu[:,c]+dot(h2,du,TN)
         R.Gd[:,c]=R.Gd[:,c]+dot(dl,a,TN)
+        between(c0//CH)
     R.bo[img]=bo.astype(R.bo.dtype)
     e=dh2*R.g2
     m1=jnp.mean(e,axis=-1,keepdims=True)
@@ -89,12 +90,10 @@
     R.gn[1:2,:]=R.gn[1:2,:]+jnp.sum(dh2*xh2,axis=0,keepdims=True)
     R.Go[...]=R.Go[...]+dot(dy.astype(bf),o,TN)
 
-def cc(img, R):
-    dy=R.dy[img]
-    dm=dy.astype(bf)
+def cc(img, slot, R):
+    dm=R.dy[img].astype(bf)
     h1=R.h1[img]
     lo=lax.broadcasted_iota(jnp.int32,(S,128),1)<64
-    dh1=jnp.zeros((S,D),f32)
     for b in range(3):
         sl=slice(128*b,128*b+128)
         do=dot(dm,R.wo[:,sl]).astype(bf)
@@ -103,21 +102,23 @@
         k=R.qkv[img,:,384+128*b:512+128*b]
         v=R.qkv[img,:,768+128*b:896+128*b]
         p=R.p[img,b]
-        dv=dot(p.astype(bf),do2).astype(bf)
+        dv=dot(p,do2).astype(bf)
+        p=p.astype(f32)
         dp=dot(v,do2,NT)
         inner=jnp.sum(p*dp,axis=0,keepdims=True)
         ds=(p*(dp-inner)).astype(bf)
         dk=dot(ds,q2).astype(bf)
         dq=(unstackT(dot(k,ds,TN))*0.125).astype(bf)
-        R.dqkv[:,sl]=dq; R.dqkv[:,384+128*b:512+128*b]=dk; R.dqkv[:,768+128*b:896+128*b]=dv
-    dqkv=R.dqkv[...]
-    R.Gqkv[...]=R.Gqkv[...]+dot(h1,dqkv,TN)
-    dh1=dot(dqkv,R.wqkv[...],NT)
-    xh1,r1=ln_stats(R.x[img])
+        R.dqkv[slot,:,sl]=dq; R.dqkv[slot,:,384+128*b:512+128*b]=dk; R.dqkv[slot,:,768+128*b:896+128*b]=dv
+    R.Gqkv[...]=R.Gqkv[...]+dot(h1,R.dqkv[slot],TN)
+
+def cc_out(img, slot, R):
+    dh1=dot(R.dqkv[slot],R.wqkv[...],NT)
+    xh1=R.xh[img]
     e=dh1*R.g1
     m1=jnp.mean(e,axis=-1,keepdims=True)
     m2=jnp.mean(e*xh1,axis=-1,keepdims=True)
-    ig=dy+r1*(e-m1-xh1*m2)
+    ig=R.dy[img]+R.r1[:,img:img+1]*(e-m1-xh1*m2)
     R.ig[img]=ig.astype(R.ig.dtype)
     R.gn[0:1,:]=R.gn[0:1,:]+jnp.sum(dh1*xh1,axis=0,keepdims=True)
 
@@ -136,7 +137,7 @@
 
 class Plan:
     def __init__(self, dp, mp, rows, images):
-        assert mp == 2 and dp >= 4 and dp & (dp - 1) == 0
+        assert mp == 2 and dp >= 8 and dp & (dp - 1) == 0
         self.dp, self.mp, self.rows = dp, mp, rows
         self.bits = dp.bit_length() - 1
         self.slots = dp * mp
@@ -144,22 +145,24 @@
         self.images = images
         self.here = images // mp
         high = [("dp", b) for b in range(2, self.bits)]
-        high = [high] if high else []
-        x, y, core = [("mp", 0)], [("dp", 1)], [("dp", 0)]
+        x, y, core = ("mp", 0), ("dp", 1), ("dp", 0)
+        split = lambda *stages: [e for e in stages if e]
         self.gather = [
-            (0, 2, high + [x, y, core]),
-            (2, 1, high + [y, x, core]),
-            (3, 4, high + [y, x, core]),
-            (7, 2, high + [x, y, core]),
+            (0, 2, split(high, [x, y], [core])),
+            (2, 1, split([x, y], high, [core])),
+            (3, 2, split(high, [x, y], [core])),
+            (5, 2, split(high, [x, y], [core])),
+            (7, 2, split([x, y], high, [core])),
         ]
         self.scatter = [
-            (0, 2, [x] + high + [y, core]),
-            (2, 1, [x, y] + high + [core]),
-            (3, 4, [x] + high + [y, core]),
-            (7, 2, [x, y] + high + [core]),
+            (0, 2, split([x], high, [y], [core])),
+            (2, 1, split([x], [y], high, [core])),
+            (3, 2, split([x], [y], high, [core])),
+            (5, 2, split([x], high, [y], [core])),
+            (7, 2, split([x], high, [y], [core])),
         ]
-        self.gains = high + [y, core]
-        self.sums = [core, y] + high + [x]
+        self.gains = split(high, [y, core])
+        self.sums = split([y, core], high, [x])
 
     def copies(self, stages):
         return sum(2 ** len(e) - 1 for e in stages)
@@ -362,61 +365,53 @@
             put(R.wu, 11, jnp.where(lo, c1[4], c0[4]))
             put(R.wd, 10, jnp.where(lo, c1[5], c0[5]))
         else:
-            put(R.wo, 0, c0[0])
-            put(R.wo, 1, jnp.where(lo, c0[1], c1[1]))
-            put(R.wo, 2, c1[0])
-            put(R.wd, 11, jnp.where(lo, c1[1], c0[1]))
+            put(R.wo, 0, c0[5])
+            put(R.wo, 1, jnp.where(lo, c0[11], c1[11]))
+            put(R.wo, 2, c1[5])
+            put(R.wd, 11, jnp.where(lo, c1[11], c0[11]))
             for n in range(5):
-                put(R.wu, n, c0[2 + n])
-                put(R.wu, 5 + n, c1[2 + n])
-                put(R.wd, n, c0[7 + n])
-                put(R.wd, 5 + n, c1[7 + n])
-
-
-def pack(plan, groups, scatters, R, core, which):
+                for j, c in enumerate((c0, c1)):
+                    put(R.wu, 2 * n + j, c[n])
+                    put(R.wd, 2 * n + j, c[6 + n])
+
+
+def pack(plan, group, scatter, R, core):
     rows = plan.rows
     lo = low_half(2 * rows)
-    first, last = (0, 3) if which == "A" else (3, 9)
+    first, size, stages = group
+    half = plan.slots // 2
     for r in range(plan.dp // 2):
         at = slice(2 * r * rows, 2 * (r + 1) * rows)
 
         def get(ref, block):
             return ref[at, 128 * block : 128 * block + 128]
 
-        def piece(j, n):
-            if which == "A":
-                if n < 3:
-                    return get(R.Gqkv, 3 * n + 2 * j)
-                own = get(R.Gqkv, 3 * (n - 3) + 1)
-                fill = get(R.Gu, 7 + n) if n < 5 else get(R.Gd, 10)
-            elif n == 0:
-                return get(R.Go, 2 * j)
-            elif n == 1:
-                own, fill = get(R.Go, 1), get(R.Gd, 11)
-            elif n < 7:
-                return get(R.Gu, n - 2 + 5 * j)
-            else:
-                return get(R.Gd, n - 7 + 5 * j)
+        def mixed(j, own, fill):
             return jnp.where(lo, own, fill) if j == 0 else jnp.where(lo, fill, own)
 
+        def pair(j, f):
+            if f < 3:
+                fill = get(R.Gu, 10 + f) if f < 2 else get(R.Gd, 10)
+                return get(R.Gqkv, 3 * f + 2 * j), mixed(j, get(R.Gqkv, 3 * f + 1), fill)
+            if f < 8:
+                return get(R.Gu, 2 * (f - 3) + j), get(R.Gd, 2 * (f - 3) + j)
+            return get(R.Go, 2 * j), mixed(j, get(R.Go, 1), get(R.Gd, 11))
+
         for j in range(2):
-            for f in range(first, last):
-                g = next(n for n, e in enumerate(groups) if e[0] <= f < e[0] + e[1])
-                lane = 128 * (f - groups[g][0])
-                n = f - first
-                top, bottom = piece(j, n), piece(j, n + last - first)
+            slot = slot_of(stages[:-1], 2 * r, j)
+            for n in range(size):
+                lane = 128 * n
+                top, bottom = pair(j, first + n)
                 even = jnp.concatenate([top[:rows], bottom[:rows]], axis=0)
                 odd = jnp.concatenate([top[rows:], bottom[rows:]], axis=0)
                 if plan.folded > 2 * rows:
                     none = jnp.zeros((plan.folded - 2 * rows, 128), f32)
                     even = jnp.concatenate([even, none], axis=0)
                     odd = jnp.concatenate([odd, none], axis=0)
-                slot = slot_of(groups[g][2][:-1], 2 * r, j)
-                half = plan.slots // 2
-                scatters[g].out[half + slot, :, lane : lane + 128] = jnp.where(
+                scatter.out[half + slot, :, lane : lane + 128] = jnp.where(
                     core == 0, odd, even
                 ).astype(bf)
-                scatters[g].total[slot, :, lane : lane + 128] = jnp.where(core == 0, even, odd)
+                scatter.total[slot, :, lane : lane + 128] = jnp.where(core == 0, even, odd)
 
 
 def own_chunk(plan, j, qkv, out_w, up, down):
@@ -434,9 +429,9 @@
         mix(qkv[1, :, 128:192], up[:, 704:768]),
         mix(qkv[2, :, 128:192], dT[:, 640:704]),
     ]
-    part_b = [oT[:, :128], mix(oT[:, 128:192], dT[:, 704:768])]
-    part_b += [up[:, 128 * n : 128 * n + 128] for n in range(5)]
+    part_b = [up[:, 128 * n : 128 * n + 128] for n in range(5)] + [oT[:, :128]]
     part_b += [dT[:, 128 * n : 128 * n + 128] for n in range(5)]
+    part_b += [mix(oT[:, 128:192], dT[:, 704:768])]
     pad = plan.folded - 2 * plan.rows
     blocks = []
     for part in (part_a, part_b):
@@ -463,7 +458,8 @@
     weights_in = take(5)
     bo_out, ig_out, grads_out, gn_out = take(4)
     weights = take(5)
-    x, g, h1, qkv, p, o, dy, dqkv = take(8)
+    x, g, h1, qkv, p, o, dqkv, xh, r1 = take(9)
+    dy = x
     wqkv, wo, wu, wd, Gqkv, Go, Gu, Gd, gn = take(9)
     bo, ig = take(2)
     ng, ns = len(plan.gather), len(plan.scatter)
@@ -508,10 +504,6 @@
     ]
     gains = Sum(place, plan.gains, gains_buf, gains_send, gains_recv)
     sums = Sum(place, plan.sums, sums_buf, sums_send, sums_recv)
-    first = [c for c, e in zip(gathers, plan.gather) if e[0] < 3]
-    second = [c for c, e in zip(gathers, plan.gather) if e[0] >= 3]
-    late = [c for c, e in zip(scatters, plan.scatter) if e[0] < 3]
-    early = [c for c, e in zip(scatters, plan.scatter) if e[0] >= 3]
 
     for c in weight_loads:
         c.wait()
@@ -523,52 +515,59 @@
 
     pl.semaphore_wait(barrier, len(partners))
 
-    stages = len(plan.gather[0][2])
-    for s in range(stages):
-        for c in first:
-            if s:
-                c.wait(s - 1)
-            c.start(s)
-        if s < len(plan.gains):
-            gains.begin(s, gains.total(s - 1) if s else mine)
-        if 0 < s < stages - 1:
-            for c in second:
-                if s > 1:
-                    c.wait(s - 2)
-                c.start(s - 1)
-        if s == 0:
-            for ref in (Gqkv, Go, Gu, Gd, gn):
-                ref[...] = jnp.zeros_like(ref)
-    rounded = gains.total(len(plan.gains) - 1)
+    ga, gx, gb, ge, gc = gathers
+    gains.begin(0, mine)
+    ga.start(0)
+    gx.start(0)
+    for ref in (Gqkv, Go, Gu, Gd, gn):
+        ref[...] = jnp.zeros_like(ref)
+
+    def step(c, s):
+        c.wait(s)
+        c.start(s + 1)
+
+    def norm_rows(n):
+        loads[2 * n].wait()
+        xh[n], r1[:, n : n + 1] = ln_stats(x[n])
+
+    step(gx, 0)
+    gains.begin(1, gains.total(0))
+    step(ga, 0)
+    gb.start(0)
+    ge.start(0)
+    gc.start(0)
+    for n in range(here // 2):
+        norm_rows(n)
+    step(ga, 1)
+    for n in range(here // 2, here):
+        norm_rows(n)
+    rounded = gains.total(1)
     R = types.SimpleNamespace(
         x=x, g=g, h1=h1, qkv=qkv, p=p, o=o, dy=dy, dqkv=dqkv, wqkv=wqkv, wo=wo, wu=wu, wd=wd,
-        Gqkv=Gqkv, Go=Go, Gu=Gu, Gd=Gd, gn=gn, bo=bo, ig=ig,
+        Gqkv=Gqkv, Go=Go, Gu=Gu, Gd=Gd, gn=gn, bo=bo, ig=ig, xh=xh, r1=r1,
     )
     R.g1 = rounded[0:1, :]
     R.g2 = rounded[1:2, :]
-    for c in loads:
-        c.wait()
-    for c in first:
-        c.wait(stages - 1)
-    for c in second:
-        c.wait(stages - 3)
-        c.start(stages - 2)
+    step(gx, 1)
+    step(gc, 0)
+    step(gb, 0)
+    step(ge, 0)
+    ga.wait(2)
+    gx.wait(2)
     unpack(plan, plan.gather, gbufs, R, "A")
-
     def attend(n, carry):
         a1(n, R, counts[j * here + n])
-
-        @pl.when(n == (here - 1) // 2)
-        def _():
-            for c in second:
-                c.wait(stages - 2)
-                c.start(stages - 1)
-
         return carry
 
-    lax.fori_loop(0, here, attend, 0)
-    for c in second:
-        c.wait(stages - 1)
+    lax.fori_loop(0, here - 1, attend, 0)
+    step(gb, 1)
+    step(ge, 1)
+    step(gc, 1)
+    a1(here - 1, R, counts[j * here + here - 1])
+    for n in range(here):
+        loads[2 * n + 1].wait()
+    for c in (gb, ge, gc):
+        c.wait(2)
     unpack(plan, plan.gather, gbufs, R, "B")
     for c in gathers + [gains]:
         c.finish()
@@ -588,50 +587,72 @@
             c.start()
         return carry
 
-    lax.fori_loop(0, here, feed, 0)
+    lax.fori_loop(0, here - 1, feed, 0)
 
     core = place.bit(("dp", 0))
-    pack(plan, plan.scatter, scatters, R, core, "B")
     top = len(plan.scatter[0][2]) - 1
-    for c in early:
-        c.start(top)
-
-    def advance(group, s):
-        for c in group:
-            c.add(s)
-            if s:
-                c.start(s - 1)
-
-    due = {0: top, here - 1: top - 1}
-
-    def back(n, carry):
-        cc(n, R)
+
+    def leave(n):
+        pack(plan, plan.scatter[n], scatters[n], R, core)
+        scatters[n].start(top)
+
+    def advance(c, s):
+        c.add(s)
+        if s:
+            c.start(s - 1)
+
+    sa, sx, sb, se, sc = scatters
+
+    def between(k):
+        if k == 0:
+            leave(2)
+        if k == 1:
+            advance(sb, top)
+            leave(3)
+
+    a2(here - 1, R, between)
+    for c in swap(here - 1, 0):
+        c.start()
+    advance(se, top)
+    leave(4)
+
+    def give(n):
+        cc_out(n, n % 2, R)
         for c in swap(n, 1):
             c.start()
-        for image, s in due.items():
-
-            @pl.when(n == image)
-            def _(s=s):
-                advance(early, s)
-
-        return carry
-
-    lax.fori_loop(0, here, back, 0)
-
-    pack(plan, plan.scatter, scatters, R, core, "A")
-    for c in late:
-        c.start(top)
+
+    for n in range(here):
+        cc(n, n % 2, R)
+        if n < here - 2:
+            give(n)
+        if n == 0:
+            advance(sc, top)
+        if n == 1:
+            advance(se, top - 1)
+        if n == 2:
+            advance(sb, top - 1)
+    leave(0)
+    leave(1)
+    advance(sc, top - 1)
+    give(here - 2)
+    advance(sa, top)
+    advance(sx, top)
+    give(here - 1)
     sums.begin(0, gn[...])
-    s_early = top - 2
-    for s in range(top, -1, -1):
-        advance(late, s)
-        step = top - s
-        value = sums.total(step)
-        if step + 1 < len(plan.sums):
-            sums.begin(step + 1, value)
-        if s_early >= 0:
-            advance(early, s_early)
-            s_early -= 1
+    advance(se, top - 2)
+    advance(sb, top - 2)
+    sums.begin(1, sums.total(0))
+    advance(sa, top - 1)
+    advance(sx, top - 1)
+    advance(sc, top - 2)
+    sums.begin(2, sums.total(1))
+    advance(sa, top - 2)
+    advance(sx, top - 2)
+    for c in (sb, se, sc):
+        advance(c, 0)
+    value = sums.total(2)
+    advance(sa, 0)
+    advance(sx, 0)
     for c, (f, size, _) in zip(scatters, plan.scatter):
         grads_out[:, 128 * f : 128 * (f + size)] = c.total[c.own]
     gn_out[...] = value
@@ -671,10 +692,11 @@
         pltpu.VMEM((here, S, D), f32),
         pltpu.VMEM((here, S, D), bf),
         pltpu.VMEM((here, S, 3 * D), bf),
-        pltpu.VMEM((here, 3, S, 2 * S), f32),
+        pltpu.VMEM((here, 3, S, 2 * S), bf),
         pltpu.VMEM((here, S, D), bf),
+        pltpu.VMEM((2, S, 3 * D), bf),
         pltpu.VMEM((here, S, D), f32),
-        pltpu.VMEM((S, 3 * D), bf),
+        pltpu.VMEM((S, 128), f32),
         pltpu.VMEM((D, 3 * D), bf),
         pltpu.VMEM((D, D), bf),
         pltpu.VMEM((D, 4 * D), bf),
@@ -742,11 +764,11 @@
         left, right = value[:, :64], value[:, 64:]
         return jnp.where(j == 0, left, right), jnp.where(j == 0, right, left)
 
-    own, fill = zip(*[split(e) for e in part_a[3:] + part_b[1:2]])
+    own, fill = zip(*[split(e) for e in part_a[3:] + part_b[11:]])
     qkv = [jnp.concatenate([part_a[n], own[n]], axis=1) for n in range(3)]
-    out_w = jnp.concatenate([part_b[0], own[3]], axis=1)
-    up = jnp.concatenate(part_b[2:7] + [fill[0], fill[1]], axis=1)
-    down = jnp.concatenate(part_b[7:12] + [fill[2], fill[3]], axis=1)
+    out_w = jnp.concatenate([part_b[5], own[3]], axis=1)
+    up = jnp.concatenate(part_b[:5] + [fill[0], fill[1]], axis=1)
+    down = jnp.concatenate(part_b[6:11] + [fill[2], fill[3]], axis=1)
     norm = pltpu.roll(sums, D - i * rows, 1)[:2, :rows]
     return qkv, out_w, up, down, norm
 

time: 115 us -> 107 us (0.930)
  Pallas kernels: 114 us -> 106 us
    pallas_call x1, Pallas kernels: 107 us -> 98.1 us  [run_layer(): pl.pallas_call(functools.partial(layer_kernel, plan), out_shape=[out(inpu...]
where the time goes in v3:
time: 107 us; the launch traced here: 106 us
  Pallas kernels  106 us (99%)
    pallas_call x1, Pallas kernels, run_layer(): pl.pallas_call(functools.partial(layer_kernel, plan), out_shape=[out(inpu...  98.1 us
    pallas_call x1, Pallas kernels, run_finish(): pl.pallas_call(functools.partial(finish_kernel, plan), out_shape=[out(bo....  7.51 us

profile of v3, /device:TPU:0, one launch (start us, length us, event | category | flops | bytes accessed | tf_op | source)
XLA Modules:
  0.0 106.4 jit_solution(18110850024014345804)
XLA Ops:
  0.7 98.1 %layer.1 = (bf16[8,384,384]{2,1,0:T(8,128)(2,1)}, bf16[8,384,384]{2,1,0:T(8,128)(2,1)}, f32[48,1152]{1,0:T(8,128)}, f32[8,384]{1,0:T(8,128)}) custom-call(s32[8]{0:T(128)} %refs_0_.1, f32[8,384,384]{2,1,0:T(8,128)} %refs_1_.1, f32[8,384,384]{2,1,0:T(8,128)} %refs_2_.1, f32[3,24,192]{2,1,0:T(8,128)} %refs_4_.1, f32[24,192]{1,0:T(8,128)} %bitcast.16, ...), custom_call_target="tpu_custom_call" | custom-call | tf_op jit(solution)/shard_map/layer/pallas_call | solution.py:725
  98.7 7.5 %finish.1 = (f32[8,384,384]{2,1,0:T(8,128)}, f32[8,384,384]{2,1,0:T(8,128)}, f32[3,24,192]{2,1,0:T(8,128)}, f32[24,192]{1,0:T(8,128)}, f32[24,768]{1,0:T(8,128)}...) custom-call(bf16[8,384,384]{2,1,0:T(8,128)(2,1)} %get-tuple-element., ...), custom_call_target="tpu_custom_call" | custom-call | tf_op jit(solution)/shard_map/finish/pallas_call | solution.py:848

commit v4 on v3

--- a/solution.py
+++ b/solution.py
@@ -631,9 +631,9 @@
             advance(se, top - 1)
         if n == 2:
             advance(sb, top - 1)
+            advance(sc, top - 1)
     leave(0)
     leave(1)
-    advance(sc, top - 1)
     give(here - 2)
     advance(sa, top)
     advance(sx, top)
@@ -801,10 +801,11 @@
         for n, (src, dst) in enumerate(zip(small_in, small))
     ]
     loads, stores = [], []
-    for n in range(n_images):
+    for n in range(n_images // 2):
+        at = pl.ds(2 * n, 2)
         for k, (src, dst) in enumerate(((bo_in, bo_out), (ig_in, ig_out))):
-            loads.append(pltpu.make_async_copy(src.at[n], low.at[k, n], in_sem.at[k, n]))
-            stores.append(pltpu.make_async_copy(full.at[k, n], dst.at[n], out_sem.at[k, n]))
+            loads.append(pltpu.make_async_copy(src.at[at], low.at[k, at], in_sem.at[k, n]))
+            stores.append(pltpu.make_async_copy(full.at[k, at], dst.at[at], out_sem.at[k, n]))
     half = len(loads) // 2
     for c in loads[:half] + small_loads + loads[half:]:
         c.start()
@@ -812,7 +813,8 @@
     def convert(n):
         k, image = n % 2, n // 2
         loads[n].wait()
-        full[k, image] = low[k, image].astype(f32)
+        at = pl.ds(2 * image, 2)
+        full[k, at] = low[k, at].astype(f32)
         stores[n].start()
 
     for n in range(half):

time: 107 us -> 106 us (level)
  no operation moved by 1% of the time
where the time goes in v4:
time: 106 us
  Pallas kernels  105 us (99%)
    pallas_call x1, Pallas kernels, run_layer(): pl.pallas_call(functools.partial(layer_kernel, plan), out_shape=[out(inpu...  98.1 us
    pallas_call x1, Pallas kernels, run_finish(): pl.pallas_call(functools.partial(finish_kernel, plan), out_shape=[out(bo....  6.77 us

profile of v4, /device:TPU:0, one launch (start us, length us, event | category | flops | bytes accessed | tf_op | source)
XLA Modules:
  0.0 105.7 jit_solution(15230236331658978890)
XLA Ops:
  0.7 98.1 %layer.1 = (bf16[8,384,384]{2,1,0:T(8,128)(2,1)}, bf16[8,384,384]{2,1,0:T(8,128)(2,1)}, f32[48,1152]{1,0:T(8,128)}, f32[8,384]{1,0:T(8,128)}) custom-call(s32[8]{0:T(128)} %refs_0_.1, f32[8,384,384]{2,1,0:T(8,128)} %refs_1_.1, f32[8,384,384]{2,1,0:T(8,128)} %refs_2_.1, f32[3,24,192]{2,1,0:T(8,128)} %refs_4_.1, f32[24,192]{1,0:T(8,128)} %bitcast.16, ...), custom_call_target="tpu_custom_call" | custom-call | tf_op jit(solution)/shard_map/layer/pallas_call | solution.py:725
  98.7 6.8 %finish.1 = (f32[8,384,384]{2,1,0:T(8,128)}, f32[8,384,384]{2,1,0:T(8,128)}, f32[3,24,192]{2,1,0:T(8,128)}, f32[24,192]{1,0:T(8,128)}, f32[24,768]{1,0:T(8,128)}...) custom-call(bf16[8,384,384]{2,1,0:T(8,128)(2,1)} %get-tuple-element., ...), custom_call_target="tpu_custom_call" | custom-call | tf_op jit(solution)/shard_map/finish/pallas_call | solution.py:850
